TPU v7x, 32 devices: a whole 2x2x4 slice. The times are simulated.
32 devices in a mesh: node: 4 (over y, x), local: 2 (over core), edata: 4 (over z).
Axes of the slice: x: 2, y: 2, z: 4, core: 2. Of those that a mesh axis runs over, the one named last changes fastest.
Arguments:
- tokens: bfloat16 [2048, 4096], P(('node', 'local'), 'edata'), may hold values from -6 to 6
- grad_out: bfloat16 [2048, 4096], P(('node', 'local'), 'edata'), may hold values from -0.59765625 to 0.59765625
- routes: int32 [2048, 2], P(('node', 'local')), may hold values from 0 to 63, all different within a row
- gates: bfloat16 [2048, 2], P(('node', 'local')), may hold values from 0.099609375 to 1
- w_in: bfloat16 [4096, 2048], P('edata', ('node', 'local')), may hold values from -0.09375 to 0.09375
- w_out: bfloat16 [2048, 4096], P(('node', 'local'), 'edata'), may hold values from -0.09375 to 0.09375
Outputs:
- grad_tokens: bfloat16 [2048, 4096], P(('node', 'local'), 'edata')
- grad_gates: float32 [2048, 2], P(('node', 'local'))
- grad_w_in: float32 [4096, 2048], P('edata', ('node', 'local'))
- grad_w_out: float32 [2048, 4096], P(('node', 'local'), 'edata')
Inputs may be any that keep to these rules, and one draw needn't show every extreme that they name: `routes`: each token names two different experts.
All inputs are finite; a program needn't handle non-finite values.
Results may differ from a plain program's by a relative error of at most 0.0049.
Values may be sent and summed in bfloat16 or wider, within the bound.
No kernel may reach another device: no remote copies, remote signals or barrier semaphores. Data moves between devices by JAX's collectives and lax.ppermute only.
A program may use at most 64 MiB of HBM per device.

v0:
```python
import functools

import jax
import jax.numpy as jnp
from jax import lax
from jax.experimental import pallas as pl
from jax.experimental.pallas import tpu as pltpu
from jax.sharding import PartitionSpec as P

EXPERTS = 64
WINDOW = 2
LANES = 128
PIECES = 4
VMEM_LIMIT = 40 * 1024 * 1024

BF16 = jnp.bfloat16
F32 = jnp.float32
I16 = jnp.int16
ROWS_BY_ROWS = (((0,), (0,)), ((), ()))
COLS_BY_COLS = (((1,), (1,)), ((), ()))


def gelu_pair(pre_act):
    coefficient = 0.7978845608028654
    square = pre_act * pre_act
    tanh_val = jnp.tanh(coefficient * (pre_act + 0.044715 * pre_act * square))
    half = 0.5 * (1.0 + tanh_val)
    activation = pre_act * half
    slopes = half + 0.5 * pre_act * (1.0 - tanh_val * tanh_val) * coefficient * (
        1.0 + 3.0 * 0.044715 * square
    )
    return (activation, slopes)


def call(kernel, out_shape, flops, moved, limit=VMEM_LIMIT, **more):
    return pl.pallas_call(
        kernel,
        out_shape=out_shape,
        compiler_params=pltpu.CompilerParams(vmem_limit_bytes=limit),
        cost_estimate=pl.CostEstimate(flops=flops, bytes_accessed=moved, transcendentals=0),
        **more,
    )


def own_expert():
    half_nodes = lax.axis_size("node") // WINDOW
    return lax.axis_index("node") // half_nodes


def split_value(value):
    high = value.astype(BF16).astype(F32)
    lane = lax.broadcasted_iota(jnp.int32, (value.shape[0], LANES), 1)
    return jnp.where(lane == 0, high, jnp.where(lane == 1, value - high, 0.0))


def encode(values):
    top = jnp.max(jnp.abs(values), axis=1, keepdims=True)
    power = jnp.ceil(jnp.log2(jnp.maximum(top, 1e-30)))
    codes = jnp.round(values * (1.999 * jnp.exp2(14.0 - power)))
    return codes.astype(jnp.int32).astype(I16), power


def decode(codes, power):
    return codes.astype(jnp.int32).astype(F32) * (jnp.exp2(power - 14.0) / 1.999)


def store_codes(out_ref, pair):
    hidden = pair[0].shape[1]
    lane = lax.broadcasted_iota(jnp.int32, (pair[0].shape[0], LANES), 1)
    powers = []
    for index, values in enumerate(pair):
        codes, power = encode(values)
        out_ref[:, index * hidden : (index + 1) * hidden] = codes
        powers.append(power)
    powers = jnp.where(lane == 0, powers[0], powers[1])
    out_ref[:, 2 * hidden :] = powers.astype(jnp.int32).astype(I16)


def load_codes(ref):
    hidden = (ref.shape[1] - LANES) // 2
    powers = ref[:, 2 * hidden :].astype(jnp.int32).astype(F32)
    return [
        decode(ref[:, index * hidden : (index + 1) * hidden], powers[:, index : index + 1])
        for index in range(2)
    ]


def gather_kernel(routes_hbm, gates_hbm, tokens_hbm, grads_hbm, own_ref, other_ref, place_ref,
                  routes_ref, gates_ref, tokens_ref, grads_ref, sems):
    tok_rows, feats = tokens_ref.shape
    capacity = own_ref.shape[0] // 2
    slots = WINDOW * capacity
    copies = [
        pltpu.make_async_copy(routes_hbm, routes_ref, sems.at[0]),
        pltpu.make_async_copy(gates_hbm, gates_ref, sems.at[1]),
    ]
    count = tok_rows // PIECES
    for source, target in ((tokens_hbm, tokens_ref), (grads_hbm, grads_ref)):
        for piece in range(PIECES):
            span = pl.ds(piece * count, count)
            copies.append(
                pltpu.make_async_copy(source.at[span], target.at[span], sems.at[len(copies)])
            )
    for copy in copies:
        copy.start()
    earlier = lax.broadcasted_iota(jnp.int32, (tok_rows, tok_rows), 0) < lax.broadcasted_iota(
        jnp.int32, (tok_rows, tok_rows), 1
    )
    earlier = earlier.astype(F32).astype(BF16)
    slot_of = lax.broadcasted_iota(jnp.int32, (capacity, tok_rows), 0).astype(F32)
    row_of = lax.broadcasted_iota(jnp.int32, (8, tok_rows), 0)
    own = own_expert()
    copies[0].wait()
    copies[1].wait()
    routes = routes_ref[...]
    gates = gates_ref[...].astype(F32)
    hits = [(routes == expert).astype(F32) for expert in (own, 1 - own)]
    named = [hit[0:1] + hit[1:2] for hit in hits]
    weight = [hit * gates for hit in hits]
    weight = [value[0:1] + value[1:2] for value in weight]
    names = jnp.where(row_of == 0, named[0], jnp.where(row_of == 1, named[1], 0.0)).astype(BF16)
    before = jnp.dot(names, earlier, preferred_element_type=F32)
    parts = [jnp.where(before[e : e + 1] == slot_of, named[e], 0.0) for e in range(WINDOW)]
    place = jnp.concatenate(parts, axis=0).astype(BF16)
    place_ref[:slots] = place
    masks = jnp.zeros((16, tok_rows), F32)
    row_of = lax.broadcasted_iota(jnp.int32, masks.shape, 0)
    for index, hit in enumerate(hits):
        for k in range(2):
            masks = jnp.where(row_of == 2 * index + k, hit[k : k + 1], masks)
    place_ref[slots:] = masks.astype(BF16)
    for copy in copies[2 : 2 + PIECES]:
        copy.wait()
    rows_x = jnp.dot(place, tokens_ref[...], preferred_element_type=F32)
    for copy in copies[2 + PIECES :]:
        copy.wait()
    rows_dy = jnp.dot(place, grads_ref[...], preferred_element_type=F32)
    for expert, out_ref in ((0, own_ref), (1, other_ref)):
        span = slice(expert * capacity, (expert + 1) * capacity)
        out_ref[:, :feats] = jnp.concatenate([rows_x[span], rows_dy[span]], axis=0).astype(BF16)
        gate = jnp.sum(parts[expert] * weight[expert], axis=1, keepdims=True)
        gate = jnp.concatenate([gate, gate], axis=0)
        out_ref[:, feats:] = jnp.broadcast_to(gate, (2 * capacity, LANES)).astype(BF16)


def join_kernel(*refs):
    *pieces, out_ref = refs
    rows = pieces[0].shape[0]
    for index, ref in enumerate(pieces):
        out_ref[index * rows : (index + 1) * rows] = ref[...]


def part_kernel(capacity, first_ref, second_ref, w_in_ref, w_out_ref, part_ref, gate_ref):
    feats, hidden = w_in_ref.shape
    rows = jnp.concatenate([first_ref[...], second_ref[...]], axis=0)
    groups = rows.shape[0] // (2 * capacity)
    gate = rows[:, feats:].astype(F32).reshape(groups, 2 * capacity, LANES)
    gate_ref[...] = gate[:, :capacity].reshape(groups * capacity, LANES)
    rows = rows[:, :feats]
    pre = jnp.dot(rows, w_in_ref[...], preferred_element_type=F32)
    back = lax.dot_general(rows, w_out_ref[...], COLS_BY_COLS, preferred_element_type=F32)
    pre = pre.reshape(groups, 2 * capacity, hidden)[:, :capacity]
    back = back.reshape(groups, 2 * capacity, hidden)[:, capacity:]
    pair = [value.reshape(groups * capacity, hidden) for value in (pre, back)]
    store_codes(part_ref, pair)


def add_codes_kernel(first_ref, second_ref, out_ref):
    pairs = zip(load_codes(first_ref), load_codes(second_ref))
    store_codes(out_ref, [first + second for first, second in pairs])


def slot_kernel(capacity, first_ref, second_ref, gate_ref, w_in_ref, keep_ref, send_ref, dpre_ref,
                act_ref):
    feats, hidden = w_in_ref.shape
    pairs = zip(load_codes(first_ref), load_codes(second_ref))
    pre, back = [first + second for first, second in pairs]
    gate = gate_ref[:, :1]
    activation, slopes = gelu_pair(pre)
    dpre = (gate * back * slopes).astype(BF16)
    act = gate * activation
    rows = dpre.shape[0]
    slot = lax.dot_general(dpre, w_in_ref[...], COLS_BY_COLS, preferred_element_type=F32)
    slot_gate = split_value(jnp.sum(activation * back, axis=1, keepdims=True))
    half = rows // 2
    keep_ref[:, :feats] = slot[:half]
    keep_ref[:, feats:] = slot_gate[:half]
    send_ref[:, :feats] = slot[half:].astype(send_ref.dtype)
    send_ref[:, feats:] = slot_gate[half:].astype(send_ref.dtype)
    groups = rows // capacity
    dpre = dpre.astype(F32).reshape(groups, capacity, hidden)
    act = act.reshape(groups, capacity, hidden)
    blank = jnp.zeros_like(dpre)
    dpre_ref[...] = jnp.concatenate([dpre, blank], axis=1).reshape(2 * rows, hidden).astype(BF16)
    act_ref[...] = jnp.concatenate([blank, act], axis=1).reshape(2 * rows, hidden).astype(BF16)


def halve_kernel(kept_ref, came_ref, keep_ref, send_ref):
    half = keep_ref.shape[0]
    total = kept_ref[...] + came_ref[...]
    keep_ref[...] = total[:half]
    send_ref[...] = total[half:]


def deal_kernel(kept_ref, came_ref, keep_ref, *send_refs):
    each, wide = keep_ref.shape
    feats = wide - LANES
    total = kept_ref[...] + came_ref[...]
    keep_ref[...] = total[:each]
    gate = split_value(jnp.sum(total[:, feats:], axis=1, keepdims=True))
    for index, send_ref in enumerate(send_refs):
        span = slice((index + 1) * each, (index + 2) * each)
        send_ref[:, :feats] = total[span, :feats].astype(BF16)
        send_ref[:, feats:] = gate[span].astype(BF16)


def w_in_kernel(first_ref, second_ref, dpre_ref, out_ref):
    feats = out_ref.shape[0]
    rows = jnp.concatenate([first_ref[:, :feats], second_ref[:, :feats]], axis=0)
    out_ref[...] = lax.dot_general(rows, dpre_ref[...], ROWS_BY_ROWS, preferred_element_type=F32)


def w_out_kernel(first_ref, second_ref, act_ref, out_ref):
    feats = out_ref.shape[1]
    rows = jnp.concatenate([first_ref[:, :feats], second_ref[:, :feats]], axis=0)
    out_ref[...] = lax.dot_general(act_ref[...], rows, ROWS_BY_ROWS, preferred_element_type=F32)


def combine_kernel(steps, *refs):
    kept_ref, came_refs = refs[0], refs[1:steps]
    place_ref, tokens_hbm, gate_out_ref, tokens_ref, sems = refs[steps:]
    tok_rows, feats = tokens_ref.shape
    capacity = kept_ref.shape[0]
    came = [ref[...].astype(F32) for ref in came_refs]
    half = steps // WINDOW
    own = sum(came[: half - 1], kept_ref[...])
    other = sum(came[half:], came[half - 1])
    slots = jnp.concatenate([own, other], axis=0)
    place = place_ref[: WINDOW * capacity]
    grads = slots[:, :feats]
    high = grads.astype(BF16)
    low = (grads - high.astype(F32)).astype(BF16)
    both = jnp.concatenate([high, low], axis=0)
    twice = jnp.concatenate([place, place], axis=0)
    count = tok_rows // PIECES
    copies = []
    for piece in range(PIECES):
        span = pl.ds(piece * count, count)
        tokens_ref[span] = lax.dot_general(
            twice[:, piece * count : (piece + 1) * count],
            both,
            ROWS_BY_ROWS,
            preferred_element_type=F32,
        ).astype(BF16)
        copy = pltpu.make_async_copy(tokens_ref.at[span], tokens_hbm.at[span], sems.at[piece])
        copy.start()
        copies.append(copy)
    slot_gate = jnp.sum(slots[:, feats:], axis=1, keepdims=True)
    picked = place.astype(F32) * slot_gate
    masks = place_ref[WINDOW * capacity :].astype(F32)
    result = jnp.zeros(gate_out_ref.shape, F32)
    for index in range(WINDOW):
        span = slice(index * capacity, (index + 1) * capacity)
        value = jnp.sum(picked[span], axis=0, keepdims=True)
        result = result + masks[2 * index : 2 * index + 2] * value
    gate_out_ref[...] = result
    for copy in copies:
        copy.wait()


def swap(array, axes, bit):
    size = lax.axis_size(axes)
    return lax.ppermute(array, axes, [(index, index ^ bit) for index in range(size)])


def body(tokens, grad_out, routes, gates, w_in, w_out):
    nodes = lax.axis_size("node")
    locals_ = lax.axis_size("local")
    edatas = lax.axis_size("edata")
    tok_rows, feats = tokens.shape
    hidden = w_in.shape[1]
    capacity = 2 * tok_rows // EXPERTS
    slots = WINDOW * capacity
    rows = nodes * locals_ * capacity
    wide = feats + LANES
    coded = 2 * hidden + LANES
    shape = jax.ShapeDtypeStruct
    hbm = pl.BlockSpec(memory_space=pltpu.HBM)
    vmem = pl.BlockSpec(memory_space=pltpu.VMEM)

    own_rows, other_rows, place = call(
        gather_kernel,
        (
            shape((2 * capacity, wide), BF16),
            shape((2 * capacity, wide), BF16),
            shape((slots + 16, tok_rows), BF16),
        ),
        4 * slots * tok_rows * feats,
        4 * tok_rows * feats,
        in_specs=[hbm] * 4,
        scratch_shapes=[
            pltpu.VMEM((2, tok_rows), jnp.int32),
            pltpu.VMEM((2, tok_rows), BF16),
            pltpu.VMEM((tok_rows, feats), BF16),
            pltpu.VMEM((tok_rows, feats), BF16),
            pltpu.SemaphoreType.DMA((2 + 2 * PIECES,)),
        ],
    )(routes.T, gates.T, tokens, grad_out)

    pieces = [own_rows]
    for step in range(1, nodes):
        pieces.append(swap(own_rows if step < nodes // WINDOW else other_rows, "node", step))
    count = nodes * 2 * capacity
    held = call(join_kernel, shape((count, wide), BF16), 0, 4 * count * wide)(*pieces)
    came = swap(held, "local", 1)
    bit = 2
    while bit < locals_:
        count = 2 * held.shape[0]
        held = call(join_kernel, shape((count, wide), BF16), 0, 4 * count * wide)(held, came)
        came = swap(held, "local", bit)
        bit *= 2

    part, gate_rows = call(
        functools.partial(part_kernel, capacity),
        (shape((rows, coded), I16), shape((rows, LANES), F32)),
        8 * rows * feats * hidden,
        4 * rows * feats + 4 * feats * hidden,
    )(held, came, w_in, w_out)
    bit = 1
    other = swap(part, "edata", bit)
    while 2 * bit < edatas:
        part = call(
            add_codes_kernel, shape((rows, coded), I16), 8 * rows * hidden, 6 * rows * coded
        )(part, other)
        bit *= 2
        other = swap(part, "edata", bit)

    half = rows // 2
    keep, send, dpre, act = call(
        functools.partial(slot_kernel, capacity),
        (
            shape((half, wide), F32),
            shape((half, wide), F32),
            shape((2 * rows, hidden), BF16),
            shape((2 * rows, hidden), BF16),
        ),
        2 * rows * feats * hidden,
        2 * feats * hidden + 2 * rows * feats,
    )(part, other, gate_rows, w_in)
    back = swap(send, "local", locals_ // 2)
    bit = locals_ // 4
    while bit:
        half //= 2
        keep, send = call(
            halve_kernel, (shape((half, wide), F32),) * 2, 4 * half * wide, 24 * half * wide
        )(keep, back)
        back = swap(send, "local", bit)
        bit //= 2
    keep, *sends = call(
        deal_kernel,
        (shape((capacity, wide), F32),) + (shape((capacity, wide), BF16),) * (nodes - 1),
        4 * half * wide,
        12 * half * wide,
    )(keep, back)
    backs = [swap(send, "node", step + 1) for step, send in enumerate(sends)]
    grad_w_in = call(
        w_in_kernel,
        shape((feats, hidden), F32),
        4 * rows * feats * hidden,
        4 * feats * hidden,
    )(held, came, dpre)
    grad_w_out = call(
        w_out_kernel,
        shape((hidden, feats), F32),
        4 * rows * feats * hidden,
        4 * feats * hidden,
    )(held, came, act)
    grad_tokens, grad_gates = call(
        functools.partial(combine_kernel, nodes),
        (shape((tok_rows, feats), BF16), shape((2, tok_rows), F32)),
        4 * slots * tok_rows * feats,
        2 * tok_rows * feats,
        in_specs=[vmem] * (nodes + 1),
        out_specs=[hbm, vmem],
        scratch_shapes=[
            pltpu.VMEM((tok_rows, feats), BF16),
            pltpu.SemaphoreType.DMA((PIECES,)),
        ],
    )(keep, *backs, place)
    return (grad_tokens, grad_gates.T, grad_w_in, grad_w_out)


def solution(mesh):
    in_specs = (
        P(("node", "local"), "edata"),
        P(("node", "local"), "edata"),
        P(("node", "local"), None),
        P(("node", "local"), None),
        P("edata", ("node", "local")),
        P(("node", "local"), "edata"),
    )
    out_specs = (
        P(("node", "local"), "edata"),
        P(("node", "local"), None),
        P("edata", ("node", "local")),
        P(("node", "local"), "edata"),
    )
    return jax.shard_map(body, mesh=mesh, in_specs=in_specs, out_specs=out_specs, check_vma=False)
```

profile of v0, /device:TPU:0, one launch (start us, length us, event | category | flops | bytes accessed | tf_op | source)
XLA Modules:
  0.0 37.3 jit_solution(6588333361249185904)
XLA Ops:
  0.6 0.0 copy-start.4
  0.6 0.0 copy-start.5
  0.7 0.7 %copy-done.4 = s32[256,2]{0,1:T(2,128)S(1)} copy-done((s32[256,2]{0,1:T(2,128)S(1)}, s32[256,2]{0,1:T(2,128)}, u32[]{:S(2)}) %copy-start.4) | copy-done | bytes 2072
  1.3 0.0 copy-done.5
  1.3 0.0 copy-start.1
  1.3 1.0 %copy-done.1 = bf16[256,1024]{1,0:T(8,128)(2,1)S(1)} copy-done((bf16[256,1024]{1,0:T(8,128)(2,1)S(1)}, bf16[256,1024]{1,0:T(8,128)(2,1)}, u32[]{:S(2)}) %copy-start.1) | copy-done | bytes 524312
  2.4 0.0 copy-start.2
  2.4 1.0 %copy-done.2 = bf16[256,1024]{1,0:T(8,128)(2,1)S(1)} copy-done((bf16[256,1024]{1,0:T(8,128)(2,1)S(1)}, bf16[256,1024]{1,0:T(8,128)(2,1)}, u32[]{:S(2)}) %copy-start.2) | copy-done | bytes 524312
  3.4 0.0 copy-start
  3.4 0.0 copy-start.3
  3.4 2.0 %shard_map.93 = (bf16[16,1152]{1,0:T(8,128)(2,1)S(1)}, bf16[16,1152]{1,0:T(8,128)(2,1)S(1)}, bf16[32,256]{1,0:T(8,128)(2,1)S(1)}) custom-call(s32[2,256]{1,0:T(2,128)S(1)} %bitcast.3, bf16[2,256]{1,0:T(2,128)(2,1)S(1)} %bitcast.4, bf16[256,1024]{1,0:T(8,128)(2,1)S(1)} %copy-done.1, bf16[256,1024]{1,0:T(8,128)(2,1)S(1)} %copy-done.2), custom_call_target="tpu_custom_call" | custom-call | flops 16777216 | bytes 1048576 | tf_op jit(solution)/shard_map/pallas_call | solution.py:291
  5.4 3.0 %collective-permute-start = (bf16[16,1152]{1,0:T(8,128)(2,1)S(1)}, bf16[16,1152]{1,0:T(8,128)(2,1)S(1)}, u32[]{:S(2)}, u32[]{:S(2)}) collective-permute-start(bf16[16,1152]{1,0:T(8,128)(2,1)S(1)} %get-tuple-element.19.refs_0_), channel_id=1, source_target_pairs={{0,8},{8,0},{16,24},{24,16},{1,9},{9,1},{17,25},{25,17},{2,10},{10... | collective-permute-start | bytes 110600 | tf_op jit(solution)/shard_map/ppermute | solution.py:273
  8.4 1.5 %collective-permute-start.1 = (bf16[16,1152]{1,0:T(8,128)(2,1)S(1)}, bf16[16,1152]{1,0:T(8,128)(2,1)S(1)}, u32[]{:S(2)}, u32[]{:S(2)}) collective-permute-start(bf16[16,1152]{1,0:T(8,128)(2,1)S(1)} %get-tuple-element.20), channel_id=1, source_target_pairs={{0,16},{8,24},{16,0},{24,8},{1,17},{9,25},{17,1},{25,9},{2,18},{10... | collective-permute-start | bytes 110600 | tf_op jit(solution)/shard_map/ppermute | solution.py:273
  10.0 0.0 collective-permute-start.2
  10.0 0.4 %collective-permute-done.refs_1_ = bf16[16,1152]{1,0:T(8,128)(2,1)S(1)} collective-permute-done((bf16[16,1152]{1,0:T(8,128)(2,1)S(1)}, bf16[16,1152]{1,0:T(8,128)(2,1)S(1)}, u32[]{:S(2)}, u32[]{:S(2)}) %collective-permute-start) | collective-permute-done | bytes 36896 | tf_op jit(solution)/shard_map/ppermute | solution.py:273
  10.4 2.0 %collective-permute-done.1.refs_2_ = bf16[16,1152]{1,0:T(8,128)(2,1)S(1)} collective-permute-done((bf16[16,1152]{1,0:T(8,128)(2,1)S(1)}, bf16[16,1152]{1,0:T(8,128)(2,1)S(1)}, u32[]{:S(2)}, u32[]{:S(2)}) %collective-permute-start.1) | collective-permute-done | bytes 36896 | tf_op jit(solution)/shard_map/ppermute | solution.py:273
  12.4 2.4 %collective-permute-done.2.refs_3_ = bf16[16,1152]{1,0:T(8,128)(2,1)S(1)} collective-permute-done((bf16[16,1152]{1,0:T(8,128)(2,1)S(1)}, bf16[16,1152]{1,0:T(8,128)(2,1)S(1)}, u32[]{:S(2)}, u32[]{:S(2)}) %collective-permute-start.2) | collective-permute-done | bytes 36896 | tf_op jit(solution)/shard_map/ppermute | solution.py:273
  14.8 0.1 collective-permute-start.3
  14.9 1.4 %collective-permute-done.3.second_ref = bf16[64,1152]{1,0:T(8,128)(2,1)S(1)} collective-permute-done((bf16[64,1152]{1,0:T(8,128)(2,1)S(1)}, bf16[64,1152]{1,0:T(8,128)(2,1)S(1)}, u32[]{:S(2)}, u32[]{:S(2)}) %collective-permute-start.3) | collective-permute-done | bytes 147488 | tf_op jit(solution)/shard_map/ppermute | solution.py:273
  16.3 0.0 copy-done
  16.3 0.0 copy-done.3
  16.3 0.5 %shard_map.95 = (s16[64,640]{1,0:T(8,128)(2,1)S(1)}, f32[64,128]{1,0:T(8,128)S(1)}) custom-call(bf16[64,1152]{1,0:T(8,128)(2,1)S(1)} %shard_map.94.first_ref, bf16[64,1152]{1,0:T(8,128)(2,1)S(1)} %collective-permute-done.3.second_ref, bf16[1024,256]{1,0:T(8,128)(2,1)S(1)} %copy-done, bf16[256,1024]{1,0:T(8,128)(2,1)S(1)} %copy-done.3), custom_call_target="tpu_custom_call" | custom-call | flops 134217728 | bytes 1310720 | tf_op jit(solution)/shard_map/pallas_call | solution.py:323
  16.7 1.6 %collective-permute-start.4 = (s16[64,640]{1,0:T(8,128)(2,1)S(1)}, s16[64,640]{1,0:T(8,128)(2,1)S(1)}, u32[]{:S(2)}, u32[]{:S(2)}) collective-permute-start(s16[64,640]{1,0:T(8,128)(2,1)S(1)} %get-tuple-element.21.first_ref), channel_id=1, source_target_pairs={{0,1},{1,0},{2,3},{3,2},{4,5},{5,4},{6,7},{7,6},{8,9},{9,8},{10,11... | collective-permute-start | bytes 245768 | tf_op jit(solution)/shard_map/ppermute | solution.py:273
  18.4 2.9 %collective-permute-done.4.second_ref = s16[64,640]{1,0:T(8,128)(2,1)S(1)} collective-permute-done((s16[64,640]{1,0:T(8,128)(2,1)S(1)}, s16[64,640]{1,0:T(8,128)(2,1)S(1)}, u32[]{:S(2)}, u32[]{:S(2)}) %collective-permute-start.4) | collective-permute-done | bytes 81952 | tf_op jit(solution)/shard_map/ppermute | solution.py:273
  21.3 0.2 shard_map.96.first_ref
  21.5 2.7 %collective-permute-start.5 = (s16[64,640]{1,0:T(8,128)(2,1)S(1)}, s16[64,640]{1,0:T(8,128)(2,1)S(1)}, u32[]{:S(2)}, u32[]{:S(2)}) collective-permute-start(s16[64,640]{1,0:T(8,128)(2,1)S(1)} %shard_map.96.first_ref), channel_id=1, source_target_pairs={{0,2},{1,3},{2,0},{3,1},{4,6},{5,7},{6,4},{7,5},{8,10},{9,11},{10,... | collective-permute-start | bytes 245768 | tf_op jit(solution)/shard_map/ppermute | solution.py:273
  24.2 3.0 %collective-permute-done.5.second_ref = s16[64,640]{1,0:T(8,128)(2,1)S(1)} collective-permute-done((s16[64,640]{1,0:T(8,128)(2,1)S(1)}, s16[64,640]{1,0:T(8,128)(2,1)S(1)}, u32[]{:S(2)}, u32[]{:S(2)}) %collective-permute-start.5) | collective-permute-done | bytes 81952 | tf_op jit(solution)/shard_map/ppermute | solution.py:273
  27.2 0.3 shard_map.97
  27.5 0.1 collective-permute-start.6
  27.6 1.4 %collective-permute-done.6.came_ref = f32[32,1152]{1,0:T(8,128)S(1)} collective-permute-done((f32[32,1152]{1,0:T(8,128)S(1)}, f32[32,1152]{1,0:T(8,128)S(1)}, u32[]{:S(2)}, u32[]{:S(2)}) %collective-permute-start.6) | collective-permute-done | bytes 147488 | tf_op jit(solution)/shard_map/ppermute | solution.py:273
  28.9 0.1 shard_map.98
  29.0 1.4 %collective-permute-start.7 = (bf16[8,1152]{1,0:T(8,128)(2,1)S(1)}, bf16[8,1152]{1,0:T(8,128)(2,1)S(1)}, u32[]{:S(2)}, u32[]{:S(2)}) collective-permute-start(bf16[8,1152]{1,0:T(8,128)(2,1)S(1)} %get-tuple-element.26), channel_id=1, source_target_pairs={{0,8},{8,0},{16,24},{24,16},{1,9},{9,1},{17,25},{25,17},{2,10},{10... | collective-permute-start | bytes 55304 | tf_op jit(solution)/shard_map/ppermute | solution.py:273
  30.4 0.5 %collective-permute-start.8 = (bf16[8,1152]{1,0:T(8,128)(2,1)S(1)}, bf16[8,1152]{1,0:T(8,128)(2,1)S(1)}, u32[]{:S(2)}, u32[]{:S(2)}) collective-permute-start(bf16[8,1152]{1,0:T(8,128)(2,1)S(1)} %get-tuple-element.27), channel_id=1, source_target_pairs={{0,16},{8,24},{16,0},{24,8},{1,17},{9,25},{17,1},{25,9},{2,18},{10... | collective-permute-start | bytes 55304 | tf_op jit(solution)/shard_map/ppermute | solution.py:273
  31.0 1.6 %collective-permute-start.9 = (bf16[8,1152]{1,0:T(8,128)(2,1)S(1)}, bf16[8,1152]{1,0:T(8,128)(2,1)S(1)}, u32[]{:S(2)}, u32[]{:S(2)}) collective-permute-start(bf16[8,1152]{1,0:T(8,128)(2,1)S(1)} %get-tuple-element.28), channel_id=1, source_target_pairs={{0,24},{8,16},{16,8},{24,0},{1,25},{9,17},{17,9},{25,1},{2,26},{10... | collective-permute-start | bytes 55304 | tf_op jit(solution)/shard_map/ppermute | solution.py:273
  32.5 1.3 %shard_map.101 = f32[256,1024]{1,0:T(8,128)} custom-call(bf16[64,1152]{1,0:T(8,128)(2,1)S(1)} %shard_map.94.first_ref, bf16[64,1152]{1,0:T(8,128)(2,1)S(1)} %collective-permute-done.3.second_ref, bf16[128,256]{1,0:T(8,128)(2,1)S(1)} %get-tuple-element.33.act_ref), custom_call_target="tpu_custom_call" | custom-call | flops 67108864 | bytes 1048576 | tf_op jit(solution)/shard_map/pallas_call | solution.py:372
  33.8 1.3 %shard_map.100 = f32[1024,256]{1,0:T(8,128)} custom-call(bf16[64,1152]{1,0:T(8,128)(2,1)S(1)} %shard_map.94.first_ref, bf16[64,1152]{1,0:T(8,128)(2,1)S(1)} %collective-permute-done.3.second_ref, bf16[128,256]{1,0:T(8,128)(2,1)S(1)} %get-tuple-element.32.dpre_ref), custom_call_target="tpu_custom_call" | custom-call | flops 67108864 | bytes 1048576 | tf_op jit(solution)/shard_map/pallas_call | solution.py:366
  35.1 0.0 collective-permute-done.7.refs_1_
  35.1 0.0 collective-permute-done.8.refs_2_
  35.1 0.5 %collective-permute-done.9.refs_3_ = bf16[8,1152]{1,0:T(8,128)(2,1)S(1)} collective-permute-done((bf16[8,1152]{1,0:T(8,128)(2,1)S(1)}, bf16[8,1152]{1,0:T(8,128)(2,1)S(1)}, u32[]{:S(2)}, u32[]{:S(2)}) %collective-permute-start.9) | collective-permute-done | bytes 18464 | tf_op jit(solution)/shard_map/ppermute | solution.py:273
  35.6 1.6 %shard_map.99 = (bf16[256,1024]{1,0:T(8,128)(2,1)}, f32[2,256]{1,0:T(2,128)}) custom-call(f32[8,1152]{1,0:T(8,128)S(1)} %get-tuple-element.25.refs_0_, bf16[8,1152]{1,0:T(8,128)(2,1)S(1)} %collective-permute-done.7.refs_1_, bf16[8,1152]{1,0:T(8,128)(2,1)S(1)} %collective-permute-done.8.refs_2_, bf16[8,1152]{1,0:T(8,128)(2,1)S(1)} %collective-permute-done.9.refs_3_, ...), custom_call_target="tpu_custom_call" | custom-call | flops 16777216 | bytes 524288 | tf_op jit(solution)/shard_map/pallas_call | solution.py:378
  (1 shorter events, 0.0 us)
Async XLA Ops:
  0.6 0.7 %copy-start.4 = (s32[256,2]{0,1:T(2,128)S(1)}, s32[256,2]{0,1:T(2,128)}, u32[]{:S(2)}) copy-start(s32[256,2]{0,1:T(2,128)} %param.8) | copy-start | bytes 6148
  0.6 0.7 %copy-start.5 = (bf16[256,2]{0,1:T(2,128)(2,1)S(1)}, bf16[256,2]{0,1:T(2,128)(2,1)}, u32[]{:S(2)}) copy-start(bf16[256,2]{0,1:T(2,128)(2,1)} %param.9) | copy-start | bytes 3076
  1.3 1.0 %copy-start.1 = (bf16[256,1024]{1,0:T(8,128)(2,1)S(1)}, bf16[256,1024]{1,0:T(8,128)(2,1)}, u32[]{:S(2)}) copy-start(bf16[256,1024]{1,0:T(8,128)(2,1)} %tokens_hbm.1) | copy-start | bytes 1572868
  2.4 1.0 %copy-start.2 = (bf16[256,1024]{1,0:T(8,128)(2,1)S(1)}, bf16[256,1024]{1,0:T(8,128)(2,1)}, u32[]{:S(2)}) copy-start(bf16[256,1024]{1,0:T(8,128)(2,1)} %grads_hbm.1) | copy-start | bytes 1572868
  3.4 12.9 %copy-start = (bf16[1024,256]{1,0:T(8,128)(2,1)S(1)}, bf16[1024,256]{1,0:T(8,128)(2,1)}, u32[]{:S(2)}) copy-start(bf16[1024,256]{1,0:T(8,128)(2,1)} %w_in_ref.3) | copy-start | bytes 1572868
  3.4 12.9 %copy-start.3 = (bf16[256,1024]{1,0:T(8,128)(2,1)S(1)}, bf16[256,1024]{1,0:T(8,128)(2,1)}, u32[]{:S(2)}) copy-start(bf16[256,1024]{1,0:T(8,128)(2,1)} %w_out_ref.1) | copy-start | bytes 1572868
  5.4 4.9 %collective-permute-start = (bf16[16,1152]{1,0:T(8,128)(2,1)S(1)}, bf16[16,1152]{1,0:T(8,128)(2,1)S(1)}, u32[]{:S(2)}, u32[]{:S(2)}) collective-permute-start(bf16[16,1152]{1,0:T(8,128)(2,1)S(1)} %get-tuple-element.19.refs_0_), channel_id=1, source_target_pairs={{0,8},{8,0},{16,24},{24,16},{1,9},{9,1},{17,25},{25,17},{2,10},{10... | collective-permute-start | bytes 110600 | tf_op jit(solution)/shard_map/ppermute | solution.py:273
  8.4 4.0 %collective-permute-start.1 = (bf16[16,1152]{1,0:T(8,128)(2,1)S(1)}, bf16[16,1152]{1,0:T(8,128)(2,1)S(1)}, u32[]{:S(2)}, u32[]{:S(2)}) collective-permute-start(bf16[16,1152]{1,0:T(8,128)(2,1)S(1)} %get-tuple-element.20), channel_id=1, source_target_pairs={{0,16},{8,24},{16,0},{24,8},{1,17},{9,25},{17,1},{25,9},{2,18},{10... | collective-permute-start | bytes 110600 | tf_op jit(solution)/shard_map/ppermute | solution.py:273
  10.0 4.9 %collective-permute-start.2 = (bf16[16,1152]{1,0:T(8,128)(2,1)S(1)}, bf16[16,1152]{1,0:T(8,128)(2,1)S(1)}, u32[]{:S(2)}, u32[]{:S(2)}) collective-permute-start(bf16[16,1152]{1,0:T(8,128)(2,1)S(1)} %get-tuple-element.20), channel_id=1, source_target_pairs={{0,24},{8,16},{16,8},{24,0},{1,25},{9,17},{17,9},{25,1},{2,26},{10... | collective-permute-start | bytes 110600 | tf_op jit(solution)/shard_map/ppermute | solution.py:273
  14.8 1.4 %collective-permute-start.3 = (bf16[64,1152]{1,0:T(8,128)(2,1)S(1)}, bf16[64,1152]{1,0:T(8,128)(2,1)S(1)}, u32[]{:S(2)}, u32[]{:S(2)}) collective-permute-start(bf16[64,1152]{1,0:T(8,128)(2,1)S(1)} %shard_map.94.first_ref), channel_id=1, source_target_pairs={{0,4},{4,0},{1,5},{5,1},{2,6},{6,2},{3,7},{7,3},{8,12},{12,8},{9,1... | collective-permute-start | bytes 442376 | tf_op jit(solution)/shard_map/ppermute | solution.py:273
  16.7 4.6 %collective-permute-start.4 = (s16[64,640]{1,0:T(8,128)(2,1)S(1)}, s16[64,640]{1,0:T(8,128)(2,1)S(1)}, u32[]{:S(2)}, u32[]{:S(2)}) collective-permute-start(s16[64,640]{1,0:T(8,128)(2,1)S(1)} %get-tuple-element.21.first_ref), channel_id=1, source_target_pairs={{0,1},{1,0},{2,3},{3,2},{4,5},{5,4},{6,7},{7,6},{8,9},{9,8},{10,11... | collective-permute-start | bytes 245768 | tf_op jit(solution)/shard_map/ppermute | solution.py:273
  21.5 5.7 %collective-permute-start.5 = (s16[64,640]{1,0:T(8,128)(2,1)S(1)}, s16[64,640]{1,0:T(8,128)(2,1)S(1)}, u32[]{:S(2)}, u32[]{:S(2)}) collective-permute-start(s16[64,640]{1,0:T(8,128)(2,1)S(1)} %shard_map.96.first_ref), channel_id=1, source_target_pairs={{0,2},{1,3},{2,0},{3,1},{4,6},{5,7},{6,4},{7,5},{8,10},{9,11},{10,... | collective-permute-start | bytes 245768 | tf_op jit(solution)/shard_map/ppermute | solution.py:273
  27.5 1.4 %collective-permute-start.6 = (f32[32,1152]{1,0:T(8,128)S(1)}, f32[32,1152]{1,0:T(8,128)S(1)}, u32[]{:S(2)}, u32[]{:S(2)}) collective-permute-start(f32[32,1152]{1,0:T(8,128)S(1)} %get-tuple-element.24), channel_id=1, source_target_pairs={{0,4},{4,0},{1,5},{5,1},{2,6},{6,2},{3,7},{7,3},{8,12},{12,8},{9,1... | collective-permute-start | bytes 442376 | tf_op jit(solution)/shard_map/ppermute | solution.py:273
  29.0 6.1 %collective-permute-start.7 = (bf16[8,1152]{1,0:T(8,128)(2,1)S(1)}, bf16[8,1152]{1,0:T(8,128)(2,1)S(1)}, u32[]{:S(2)}, u32[]{:S(2)}) collective-permute-start(bf16[8,1152]{1,0:T(8,128)(2,1)S(1)} %get-tuple-element.26), channel_id=1, source_target_pairs={{0,8},{8,0},{16,24},{24,16},{1,9},{9,1},{17,25},{25,17},{2,10},{10... | collective-permute-start | bytes 55304 | tf_op jit(solution)/shard_map/ppermute | solution.py:273
  30.4 4.7 %collective-permute-start.8 = (bf16[8,1152]{1,0:T(8,128)(2,1)S(1)}, bf16[8,1152]{1,0:T(8,128)(2,1)S(1)}, u32[]{:S(2)}, u32[]{:S(2)}) collective-permute-start(bf16[8,1152]{1,0:T(8,128)(2,1)S(1)} %get-tuple-element.27), channel_id=1, source_target_pairs={{0,16},{8,24},{16,0},{24,8},{1,17},{9,25},{17,1},{25,9},{2,18},{10... | collective-permute-start | bytes 55304 | tf_op jit(solution)/shard_map/ppermute | solution.py:273
  31.0 4.7 %collective-permute-start.9 = (bf16[8,1152]{1,0:T(8,128)(2,1)S(1)}, bf16[8,1152]{1,0:T(8,128)(2,1)S(1)}, u32[]{:S(2)}, u32[]{:S(2)}) collective-permute-start(bf16[8,1152]{1,0:T(8,128)(2,1)S(1)} %get-tuple-element.28), channel_id=1, source_target_pairs={{0,24},{8,16},{16,8},{24,0},{1,25},{9,17},{17,9},{25,1},{2,26},{10... | collective-permute-start | bytes 55304 | tf_op jit(solution)/shard_map/ppermute | solution.py:273
where the time goes:
time: 37.5 us; the launch traced here: 37.3 us
  waiting for transfers between devices  14 us (37%)
  starting transfers between devices  12.5 us (33%)
  Pallas kernels  7.29 us (19%)
  local copies, waits for them, and re-layouts  2.77 us (7%)
  between operations  0.71 us (2%)
    ppermute x10, waiting for transfers between devices, swap(): lax.ppermute(array, axes, [(index, index ^ bit) for index in range(size)])  14 us
    ppermute x10, starting transfers between devices, swap(): lax.ppermute(array, axes, [(index, index ^ bit) for index in range(size)])  12.5 us
    unnamed x12, local copies, waits for them, and re-layouts  2.77 us
    pallas_call x1, Pallas kernels, body(): call(gather_kernel, (shape((2 * capacity, wide), BF16), shape((2 * capaci...  2 us
    pallas_call x1, Pallas kernels, body(): call(functools.partial(combine_kernel, nodes), (shape((tok_rows, feats),...  1.64 us
    pallas_call x1, Pallas kernels, body(): call(w_in_kernel, shape((feats, hidden), F32), 4 * rows * feats * hidden,...  1.29 us
    pallas_call x1, Pallas kernels, body(): call(w_out_kernel, shape((hidden, feats), F32), 4 * rows * feats * hidden...  1.28 us
  transfers between devices with their start and end apart: 10, of which 8 were waited for; matrix products, arithmetic and copies ran while one was open for 0% of the time, Pallas kernels for 7%

commit v1 on v0

--- a/solution.py
+++ b/solution.py
@@ -32,14 +32,19 @@
     return (activation, slopes)
 
 
-def call(kernel, out_shape, flops, moved, limit=VMEM_LIMIT, **more):
-    return pl.pallas_call(
-        kernel,
-        out_shape=out_shape,
-        compiler_params=pltpu.CompilerParams(vmem_limit_bytes=limit),
-        cost_estimate=pl.CostEstimate(flops=flops, bytes_accessed=moved, transcendentals=0),
-        **more,
-    )
+def call(kernel, out_shape, flops, moved, limit=VMEM_LIMIT, in_specs=None, after=(), **more):
+    def run(*operands):
+        given = in_specs or [pl.BlockSpec(memory_space=pltpu.VMEM)] * len(operands)
+        return pl.pallas_call(
+            lambda *refs: kernel(*refs[len(after) :]),
+            out_shape=out_shape,
+            in_specs=[pl.BlockSpec(memory_space=pl.ANY)] * len(after) + list(given),
+            compiler_params=pltpu.CompilerParams(vmem_limit_bytes=limit),
+            cost_estimate=pl.CostEstimate(flops=flops, bytes_accessed=moved, transcendentals=0),
+            **more,
+        )(*after, *operands)
+
+    return run
 
 
 def own_expert():
@@ -86,7 +91,7 @@
 
 
 def gather_kernel(routes_hbm, gates_hbm, tokens_hbm, grads_hbm, own_ref, other_ref, place_ref,
-                  routes_ref, gates_ref, tokens_ref, grads_ref, sems):
+                  spread_ref, routes_ref, gates_ref, tokens_ref, grads_ref, sems):
     tok_rows, feats = tokens_ref.shape
     capacity = own_ref.shape[0] // 2
     slots = WINDOW * capacity
@@ -123,6 +128,7 @@
     parts = [jnp.where(before[e : e + 1] == slot_of, named[e], 0.0) for e in range(WINDOW)]
     place = jnp.concatenate(parts, axis=0).astype(BF16)
     place_ref[:slots] = place
+    spread_ref[...] = jnp.concatenate(parts + parts, axis=0).T.astype(BF16)
     masks = jnp.zeros((16, tok_rows), F32)
     row_of = lax.broadcasted_iota(jnp.int32, masks.shape, 0)
     for index, hit in enumerate(hits):
@@ -150,19 +156,17 @@
         out_ref[index * rows : (index + 1) * rows] = ref[...]
 
 
-def part_kernel(capacity, first_ref, second_ref, w_in_ref, w_out_ref, part_ref, gate_ref):
+def part_kernel(capacity, rows_ref, w_in_ref, w_out_ref, part_ref, gate_ref):
     feats, hidden = w_in_ref.shape
-    rows = jnp.concatenate([first_ref[...], second_ref[...]], axis=0)
-    groups = rows.shape[0] // (2 * capacity)
-    gate = rows[:, feats:].astype(F32).reshape(groups, 2 * capacity, LANES)
+    groups = rows_ref.shape[0] // (2 * capacity)
+    gate = rows_ref[:, feats:].astype(F32).reshape(groups, 2 * capacity, LANES)
     gate_ref[...] = gate[:, :capacity].reshape(groups * capacity, LANES)
-    rows = rows[:, :feats]
+    rows = rows_ref[:, :feats]
     pre = jnp.dot(rows, w_in_ref[...], preferred_element_type=F32)
     back = lax.dot_general(rows, w_out_ref[...], COLS_BY_COLS, preferred_element_type=F32)
     pre = pre.reshape(groups, 2 * capacity, hidden)[:, :capacity]
     back = back.reshape(groups, 2 * capacity, hidden)[:, capacity:]
-    pair = [value.reshape(groups * capacity, hidden) for value in (pre, back)]
-    store_codes(part_ref, pair)
+    store_codes(part_ref, [value.reshape(groups * capacity, hidden) for value in (pre, back)])
 
 
 def add_codes_kernel(first_ref, second_ref, out_ref):
@@ -170,8 +174,7 @@
     store_codes(out_ref, [first + second for first, second in pairs])
 
 
-def slot_kernel(capacity, first_ref, second_ref, gate_ref, w_in_ref, keep_ref, send_ref, dpre_ref,
-                act_ref):
+def slot_kernel(capacity, first_ref, second_ref, gate_ref, w_in_ref, slot_ref, dpre_ref, act_ref):
     feats, hidden = w_in_ref.shape
     pairs = zip(load_codes(first_ref), load_codes(second_ref))
     pre, back = [first + second for first, second in pairs]
@@ -180,13 +183,10 @@
     dpre = (gate * back * slopes).astype(BF16)
     act = gate * activation
     rows = dpre.shape[0]
-    slot = lax.dot_general(dpre, w_in_ref[...], COLS_BY_COLS, preferred_element_type=F32)
-    slot_gate = split_value(jnp.sum(activation * back, axis=1, keepdims=True))
-    half = rows // 2
-    keep_ref[:, :feats] = slot[:half]
-    keep_ref[:, feats:] = slot_gate[:half]
-    send_ref[:, :feats] = slot[half:].astype(send_ref.dtype)
-    send_ref[:, feats:] = slot_gate[half:].astype(send_ref.dtype)
+    slot_ref[:, :feats] = lax.dot_general(
+        dpre, w_in_ref[...], COLS_BY_COLS, preferred_element_type=F32
+    )
+    slot_ref[:, feats:] = split_value(jnp.sum(activation * back, axis=1, keepdims=True))
     groups = rows // capacity
     dpre = dpre.astype(F32).reshape(groups, capacity, hidden)
     act = act.reshape(groups, capacity, hidden)
@@ -214,49 +214,59 @@
         send_ref[:, feats:] = gate[span].astype(BF16)
 
 
-def w_in_kernel(first_ref, second_ref, dpre_ref, out_ref):
-    feats = out_ref.shape[0]
-    rows = jnp.concatenate([first_ref[:, :feats], second_ref[:, :feats]], axis=0)
-    out_ref[...] = lax.dot_general(rows, dpre_ref[...], ROWS_BY_ROWS, preferred_element_type=F32)
-
-
-def w_out_kernel(first_ref, second_ref, act_ref, out_ref):
-    feats = out_ref.shape[1]
-    rows = jnp.concatenate([first_ref[:, :feats], second_ref[:, :feats]], axis=0)
-    out_ref[...] = lax.dot_general(act_ref[...], rows, ROWS_BY_ROWS, preferred_element_type=F32)
+def weight_kernel(held_ref, came_ref, dpre_held_ref, dpre_came_ref, act_held_ref, act_came_ref,
+                  w_in_hbm, w_out_hbm, w_in_ref, w_out_ref, sems):
+    feats, hidden = w_in_ref.shape
+    rows = jnp.concatenate([held_ref[:, :feats], came_ref[:, :feats]], axis=0)
+    dpre = jnp.concatenate([dpre_held_ref[...], dpre_came_ref[...]], axis=0)
+    act = jnp.concatenate([act_held_ref[...], act_came_ref[...]], axis=0)
+    count = feats // PIECES
+    copies = []
+    for piece in range(PIECES):
+        span = slice(piece * count, (piece + 1) * count)
+        part = rows[:, span]
+        w_in_ref[span] = lax.dot_general(part, dpre, ROWS_BY_ROWS, preferred_element_type=F32)
+        w_out_ref[:, span] = lax.dot_general(act, part, ROWS_BY_ROWS, preferred_element_type=F32)
+        span = pl.ds(piece * count, count)
+        for source, target in (
+            (w_in_ref.at[span], w_in_hbm.at[span]),
+            (w_out_ref.at[:, span], w_out_hbm.at[:, span]),
+        ):
+            copy = pltpu.make_async_copy(source, target, sems.at[len(copies)])
+            copy.start()
+            copies.append(copy)
+    for copy in copies:
+        copy.wait()
 
 
 def combine_kernel(steps, *refs):
     kept_ref, came_refs = refs[0], refs[1:steps]
-    place_ref, tokens_hbm, gate_out_ref, tokens_ref, sems = refs[steps:]
-    tok_rows, feats = tokens_ref.shape
+    place_ref, spread_ref, tokens_hbm, gate_out_ref, tokens_ref, sems = refs[steps:]
+    feats = tokens_ref.shape[1]
     capacity = kept_ref.shape[0]
     came = [ref[...].astype(F32) for ref in came_refs]
     half = steps // WINDOW
     own = sum(came[: half - 1], kept_ref[...])
     other = sum(came[half:], came[half - 1])
     slots = jnp.concatenate([own, other], axis=0)
-    place = place_ref[: WINDOW * capacity]
     grads = slots[:, :feats]
     high = grads.astype(BF16)
     low = (grads - high.astype(F32)).astype(BF16)
     both = jnp.concatenate([high, low], axis=0)
-    twice = jnp.concatenate([place, place], axis=0)
-    count = tok_rows // PIECES
+    spread = spread_ref[...]
+    count = feats // PIECES
     copies = []
     for piece in range(PIECES):
+        span = slice(piece * count, (piece + 1) * count)
+        tokens_ref[:, span] = jnp.dot(
+            spread, both[:, span], preferred_element_type=F32
+        ).astype(BF16)
         span = pl.ds(piece * count, count)
-        tokens_ref[span] = lax.dot_general(
-            twice[:, piece * count : (piece + 1) * count],
-            both,
-            ROWS_BY_ROWS,
-            preferred_element_type=F32,
-        ).astype(BF16)
-        copy = pltpu.make_async_copy(tokens_ref.at[span], tokens_hbm.at[span], sems.at[piece])
+        copy = pltpu.make_async_copy(tokens_ref.at[:, span], tokens_hbm.at[:, span], sems.at[piece])
         copy.start()
         copies.append(copy)
     slot_gate = jnp.sum(slots[:, feats:], axis=1, keepdims=True)
-    picked = place.astype(F32) * slot_gate
+    picked = place_ref[: WINDOW * capacity].astype(F32) * slot_gate
     masks = place_ref[WINDOW * capacity :].astype(F32)
     result = jnp.zeros(gate_out_ref.shape, F32)
     for index in range(WINDOW):
@@ -271,6 +281,12 @@
 def swap(array, axes, bit):
     size = lax.axis_size(axes)
     return lax.ppermute(array, axes, [(index, index ^ bit) for index in range(size)])
+
+
+def join(pieces):
+    rows, wide = pieces[0].shape
+    rows *= len(pieces)
+    return call(join_kernel, jax.ShapeDtypeStruct((rows, wide), BF16), 0, 4 * rows * wide)(*pieces)
 
 
 def body(tokens, grad_out, routes, gates, w_in, w_out):
@@ -288,12 +304,17 @@
     hbm = pl.BlockSpec(memory_space=pltpu.HBM)
     vmem = pl.BlockSpec(memory_space=pltpu.VMEM)
 
-    own_rows, other_rows, place = call(
+    routes_t, gates_t, tokens, grad_out = [
+        pltpu.with_memory_space_constraint(value, pltpu.HBM)
+        for value in (routes.T, gates.T, tokens, grad_out)
+    ]
+    own_rows, other_rows, place, spread = call(
         gather_kernel,
         (
-            shape((2 * capacity, wide), BF16),
-            shape((2 * capacity, wide), BF16),
-            shape((slots + 16, tok_rows), BF16),
+            pltpu.VMEM((2 * capacity, wide), BF16),
+            pltpu.VMEM((2 * capacity, wide), BF16),
+            pltpu.VMEM((slots + 16, tok_rows), BF16),
+            pltpu.VMEM((tok_rows, 2 * slots), BF16),
         ),
         4 * slots * tok_rows * feats,
         4 * tok_rows * feats,
@@ -305,48 +326,64 @@
             pltpu.VMEM((tok_rows, feats), BF16),
             pltpu.SemaphoreType.DMA((2 + 2 * PIECES,)),
         ],
-    )(routes.T, gates.T, tokens, grad_out)
-
-    pieces = [own_rows]
-    for step in range(1, nodes):
-        pieces.append(swap(own_rows if step < nodes // WINDOW else other_rows, "node", step))
-    count = nodes * 2 * capacity
-    held = call(join_kernel, shape((count, wide), BF16), 0, 4 * count * wide)(*pieces)
+    )(routes_t, gates_t, tokens, grad_out)
+
+    pieces = [own_rows] * nodes
+    for step in reversed(range(1, nodes)):
+        pieces[step] = swap(own_rows if step < nodes // WINDOW else other_rows, "node", step)
+    held = join(pieces)
     came = swap(held, "local", 1)
     bit = 2
     while bit < locals_:
-        count = 2 * held.shape[0]
-        held = call(join_kernel, shape((count, wide), BF16), 0, 4 * count * wide)(held, came)
+        held = join([held, came])
         came = swap(held, "local", bit)
         bit *= 2
 
-    part, gate_rows = call(
-        functools.partial(part_kernel, capacity),
-        (shape((rows, coded), I16), shape((rows, LANES), F32)),
-        8 * rows * feats * hidden,
-        4 * rows * feats + 4 * feats * hidden,
-    )(held, came, w_in, w_out)
-    bit = 1
-    other = swap(part, "edata", bit)
-    while 2 * bit < edatas:
-        part = call(
-            add_codes_kernel, shape((rows, coded), I16), 8 * rows * hidden, 6 * rows * coded
-        )(part, other)
+    half = rows // 2
+    last = ()
+    sums = []
+    for chunk in (held, came):
+        part, gate_rows = call(
+            functools.partial(part_kernel, capacity),
+            (shape((half, coded), I16), shape((half, LANES), F32)),
+            8 * half * feats * hidden,
+            4 * half * feats + 4 * feats * hidden,
+            after=last,
+        )(chunk, w_in, w_out)
+        last = (part,)
+        sums.append([part, swap(part, "edata", 1), gate_rows])
+    bit = 2
+    while bit < edatas:
+        for index, (part, other, gate_rows) in enumerate(sums):
+            part = call(
+                add_codes_kernel,
+                shape((half, coded), I16),
+                8 * half * hidden,
+                6 * half * coded,
+                after=last,
+            )(part, other)
+            last = (part,)
+            sums[index] = [part, swap(part, "edata", bit), gate_rows]
         bit *= 2
-        other = swap(part, "edata", bit)
-
-    half = rows // 2
-    keep, send, dpre, act = call(
-        functools.partial(slot_kernel, capacity),
-        (
-            shape((half, wide), F32),
-            shape((half, wide), F32),
-            shape((2 * rows, hidden), BF16),
-            shape((2 * rows, hidden), BF16),
-        ),
-        2 * rows * feats * hidden,
-        2 * feats * hidden + 2 * rows * feats,
-    )(part, other, gate_rows, w_in)
+    slot_parts = []
+    operands = []
+    for part, other, gate_rows in sums:
+        slot, dpre, act = call(
+            functools.partial(slot_kernel, capacity),
+            (
+                shape((half, wide), F32),
+                shape((2 * half, hidden), BF16),
+                shape((2 * half, hidden), BF16),
+            ),
+            2 * half * feats * hidden,
+            2 * feats * hidden + 4 * half * feats,
+            after=last,
+        )(part, other, gate_rows, w_in)
+        last = (dpre,)
+        slot_parts.append(slot)
+        operands.append((dpre, act))
+
+    keep, send = slot_parts
     back = swap(send, "local", locals_ // 2)
     bit = locals_ // 4
     while bit:
@@ -362,31 +399,33 @@
         4 * half * wide,
         12 * half * wide,
     )(keep, back)
-    backs = [swap(send, "node", step + 1) for step, send in enumerate(sends)]
-    grad_w_in = call(
-        w_in_kernel,
-        shape((feats, hidden), F32),
-        4 * rows * feats * hidden,
-        4 * feats * hidden,
-    )(held, came, dpre)
-    grad_w_out = call(
-        w_out_kernel,
-        shape((hidden, feats), F32),
-        4 * rows * feats * hidden,
-        4 * feats * hidden,
-    )(held, came, act)
+    backs = [swap(send, "node", step + 1) for step, send in reversed(list(enumerate(sends)))]
+    (dpre_held, act_held), (dpre_came, act_came) = operands
+    grad_w_in, grad_w_out = call(
+        weight_kernel,
+        (shape((feats, hidden), F32), shape((hidden, feats), F32)),
+        8 * rows * feats * hidden,
+        8 * feats * hidden,
+        in_specs=[vmem] * 6,
+        out_specs=[hbm] * 2,
+        scratch_shapes=[
+            pltpu.VMEM((feats, hidden), F32),
+            pltpu.VMEM((hidden, feats), F32),
+            pltpu.SemaphoreType.DMA((2 * PIECES,)),
+        ],
+    )(held, came, dpre_held, dpre_came, act_held, act_came)
     grad_tokens, grad_gates = call(
         functools.partial(combine_kernel, nodes),
         (shape((tok_rows, feats), BF16), shape((2, tok_rows), F32)),
         4 * slots * tok_rows * feats,
         2 * tok_rows * feats,
-        in_specs=[vmem] * (nodes + 1),
+        in_specs=[vmem] * (nodes + 2),
         out_specs=[hbm, vmem],
         scratch_shapes=[
             pltpu.VMEM((tok_rows, feats), BF16),
             pltpu.SemaphoreType.DMA((PIECES,)),
         ],
-    )(keep, *backs, place)
+    )(keep, *reversed(backs), place, spread)
     return (grad_tokens, grad_gates.T, grad_w_in, grad_w_out)
 
 

time: 37.5 us -> 33.7 us (0.90)
  waiting for transfers between devices: 14 us -> 10.6 us
  starting transfers between devices: 12.5 us -> 15.4 us
  local copies, waits for them, and re-layouts: 2.77 us -> 0.01 us
  Pallas kernels: 7.29 us -> 6.86 us
    ppermute x10 -> x12, waiting for transfers between devices: 14 us -> 10.6 us  [swap(): lax.ppermute(array, axes, [(index, index ^ bit) for index in range(size)])]
    ppermute x10 -> x12, starting transfers between devices: 12.5 us -> 15.4 us  [swap(): lax.ppermute(array, axes, [(index, index ^ bit) for index in range(size)])]
    unnamed x12 -> x4, local copies, waits for them, and re-layouts: 2.77 us -> 0.01 us
    pallas_call x9 -> x11, Pallas kernels: 7.29 us -> 6.86 us  [run(): pl.pallas_call(lambda *refs: kernel(*refs[len(after):]), out_shape=out_sh...]
  transfers between devices with their start and end apart: 10 -> 12, of which waited for: 8 -> 8; matrix products, arithmetic and copies ran while one was open for 0% -> 0% of each run, Pallas kernels for 7% -> 10%
where the time goes in v1:
time: 33.7 us; the launch traced here: 33.6 us
  starting transfers between devices  15.4 us (46%)
  waiting for transfers between devices  10.6 us (31%)
  Pallas kernels  6.86 us (20%)
  between operations  0.74 us (2%)
    ppermute x12, starting transfers between devices, swap(): lax.ppermute(array, axes, [(index, index ^ bit) for index in range(size)])  15.4 us
    ppermute x12, waiting for transfers between devices, swap(): lax.ppermute(array, axes, [(index, index ^ bit) for index in range(size)])  10.6 us
    pallas_call x11, Pallas kernels, run(): pl.pallas_call(lambda *refs: kernel(*refs[len(after):]), out_shape=out_sh...  6.86 us
  transfers between devices with their start and end apart: 12, of which 8 were waited for; matrix products, arithmetic and copies ran while one was open for 0% of the time, Pallas kernels for 10%

profile of v1, /device:TPU:0, one launch (start us, length us, event | category | flops | bytes accessed | tf_op | source)
XLA Modules:
  0.0 33.6 jit_solution(11540282714028667232)
XLA Ops:
  0.6 0.0 copy-start
  0.6 0.0 copy-start.1
  0.7 1.7 %shard_map.93 = (bf16[16,1152]{1,0:T(8,128)(2,1)S(1)}, bf16[16,1152]{1,0:T(8,128)(2,1)S(1)}, bf16[32,256]{1,0:T(8,128)(2,1)S(1)}, bf16[256,32]{1,0:T(8,128)(2,1)S(1)}) custom-call(s32[2,256]{1,0:T(2,128)} %bitcast.3, bf16[2,256]{1,0:T(2,128)(2,1)} %bitcast.4, bf16[256,1024]{1,0:T(8,128)(2,1)} %refs_2_.3, bf16[256,1024]{1,0:T(8,128)(2,1)} %refs_3_.2), custom_call_target="tpu_custom_call" | custom-call | flops 16777216 | bytes 1048576 | tf_op jit(solution)/shard_map/pallas_call | solution.py:38
  2.4 3.0 %collective-permute-start = (bf16[16,1152]{1,0:T(8,128)(2,1)S(1)}, bf16[16,1152]{1,0:T(8,128)(2,1)S(1)}, u32[]{:S(2)}, u32[]{:S(2)}) collective-permute-start(bf16[16,1152]{1,0:T(8,128)(2,1)S(1)} %get-tuple-element.26.refs_0_), channel_id=1, source_target_pairs={{0,8},{8,0},{16,24},{24,16},{1,9},{9,1},{17,25},{25,17},{2,10},{10... | collective-permute-start | bytes 110600 | tf_op jit(solution)/shard_map/ppermute | solution.py:283
  5.4 1.5 %collective-permute-start.1 = (bf16[16,1152]{1,0:T(8,128)(2,1)S(1)}, bf16[16,1152]{1,0:T(8,128)(2,1)S(1)}, u32[]{:S(2)}, u32[]{:S(2)}) collective-permute-start(bf16[16,1152]{1,0:T(8,128)(2,1)S(1)} %get-tuple-element.27), channel_id=1, source_target_pairs={{0,16},{8,24},{16,0},{24,8},{1,17},{9,25},{17,1},{25,9},{2,18},{10... | collective-permute-start | bytes 110600 | tf_op jit(solution)/shard_map/ppermute | solution.py:283
  6.9 0.0 collective-permute-start.2
  6.9 0.4 %collective-permute-done.refs_1_ = bf16[16,1152]{1,0:T(8,128)(2,1)S(1)} collective-permute-done((bf16[16,1152]{1,0:T(8,128)(2,1)S(1)}, bf16[16,1152]{1,0:T(8,128)(2,1)S(1)}, u32[]{:S(2)}, u32[]{:S(2)}) %collective-permute-start) | collective-permute-done | bytes 36896 | tf_op jit(solution)/shard_map/ppermute | solution.py:283
  7.3 2.0 %collective-permute-done.1.refs_2_ = bf16[16,1152]{1,0:T(8,128)(2,1)S(1)} collective-permute-done((bf16[16,1152]{1,0:T(8,128)(2,1)S(1)}, bf16[16,1152]{1,0:T(8,128)(2,1)S(1)}, u32[]{:S(2)}, u32[]{:S(2)}) %collective-permute-start.1) | collective-permute-done | bytes 36896 | tf_op jit(solution)/shard_map/ppermute | solution.py:283
  9.3 2.4 %collective-permute-done.2.refs_3_ = bf16[16,1152]{1,0:T(8,128)(2,1)S(1)} collective-permute-done((bf16[16,1152]{1,0:T(8,128)(2,1)S(1)}, bf16[16,1152]{1,0:T(8,128)(2,1)S(1)}, u32[]{:S(2)}, u32[]{:S(2)}) %collective-permute-start.2) | collective-permute-done | bytes 36896 | tf_op jit(solution)/shard_map/ppermute | solution.py:283
  11.7 0.1 collective-permute-start.3
  11.8 0.0 copy-done
  11.8 0.0 copy-done.1
  11.8 0.5 %shard_map.95 = (s16[32,640]{1,0:T(8,128)(2,1)S(1)}, f32[32,128]{1,0:T(8,128)S(1)}) custom-call(bf16[64,1152]{1,0:T(8,128)(2,1)S(1)} %shard_map.94.refs_0_, bf16[1024,256]{1,0:T(8,128)(2,1)S(1)} %copy-done, bf16[256,1024]{1,0:T(8,128)(2,1)S(1)} %copy-done.1), custom_call_target="tpu_custom_call" | custom-call | flops 67108864 | bytes 1179648 | tf_op jit(solution)/shard_map/pallas_call | solution.py:38
  12.3 1.6 %collective-permute-start.4 = (s16[32,640]{1,0:T(8,128)(2,1)S(1)}, s16[32,640]{1,0:T(8,128)(2,1)S(1)}, u32[]{:S(2)}, u32[]{:S(2)}) collective-permute-start(s16[32,640]{1,0:T(8,128)(2,1)S(1)} %get-tuple-element.28.refs_0_.refs_1_), channel_id=1, source_target_pairs={{0,1},{1,0},{2,3},{3,2},{4,5},{5,4},{6,7},{7,6},{8,9},{9,8},{10,11... | collective-permute-start | bytes 122888 | tf_op jit(solution)/shard_map/ppermute | solution.py:283
  14.0 0.0 collective-permute-done.3.refs_1_
  14.0 0.5 %shard_map.96 = (s16[32,640]{1,0:T(8,128)(2,1)S(1)}, f32[32,128]{1,0:T(8,128)S(1)}) custom-call(s16[32,640]{1,0:T(8,128)(2,1)S(1)} %get-tuple-element.28.refs_0_.refs_1_, bf16[64,1152]{1,0:T(8,128)(2,1)S(1)} %collective-permute-done.3.refs_1_, bf16[1024,256]{1,0:T(8,128)(2,1)S(1)} %copy-done, bf16[256,1024]{1,0:T(8,128)(2,1)S(1)} %copy-done.1), custom_call_target="tpu_custom_call" | custom-call | flops 67108864 | bytes 1179648 | tf_op jit(solution)/shard_map/pallas_call | solution.py:38
  14.4 0.9 %collective-permute-start.5 = (s16[32,640]{1,0:T(8,128)(2,1)S(1)}, s16[32,640]{1,0:T(8,128)(2,1)S(1)}, u32[]{:S(2)}, u32[]{:S(2)}) collective-permute-start(s16[32,640]{1,0:T(8,128)(2,1)S(1)} %get-tuple-element.29.refs_0_.refs_1_), channel_id=1, source_target_pairs={{0,1},{1,0},{2,3},{3,2},{4,5},{5,4},{6,7},{7,6},{8,9},{9,8},{10,11... | collective-permute-start | bytes 122888 | tf_op jit(solution)/shard_map/ppermute | solution.py:283
  15.3 1.1 %collective-permute-done.4.refs_2_ = s16[32,640]{1,0:T(8,128)(2,1)S(1)} collective-permute-done((s16[32,640]{1,0:T(8,128)(2,1)S(1)}, s16[32,640]{1,0:T(8,128)(2,1)S(1)}, u32[]{:S(2)}, u32[]{:S(2)}) %collective-permute-start.4) | collective-permute-done | bytes 40992 | tf_op jit(solution)/shard_map/ppermute | solution.py:283
  16.4 0.2 shard_map.97.refs_0_.refs_1_
  16.6 2.7 %collective-permute-start.6 = (s16[32,640]{1,0:T(8,128)(2,1)S(1)}, s16[32,640]{1,0:T(8,128)(2,1)S(1)}, u32[]{:S(2)}, u32[]{:S(2)}) collective-permute-start(s16[32,640]{1,0:T(8,128)(2,1)S(1)} %shard_map.97.refs_0_.refs_1_), channel_id=1, source_target_pairs={{0,2},{1,3},{2,0},{3,1},{4,6},{5,7},{6,4},{7,5},{8,10},{9,11},{10,... | collective-permute-start | bytes 122888 | tf_op jit(solution)/shard_map/ppermute | solution.py:283
  19.2 0.0 collective-permute-done.5.refs_2_
  19.2 0.2 shard_map.98.refs_0_.refs_1_
  19.4 2.0 %collective-permute-start.7 = (s16[32,640]{1,0:T(8,128)(2,1)S(1)}, s16[32,640]{1,0:T(8,128)(2,1)S(1)}, u32[]{:S(2)}, u32[]{:S(2)}) collective-permute-start(s16[32,640]{1,0:T(8,128)(2,1)S(1)} %shard_map.98.refs_0_.refs_1_), channel_id=1, source_target_pairs={{0,2},{1,3},{2,0},{3,1},{4,6},{5,7},{6,4},{7,5},{8,10},{9,11},{10,... | collective-permute-start | bytes 122888 | tf_op jit(solution)/shard_map/ppermute | solution.py:283
  21.5 0.1 collective-permute-done.6.refs_2_
  21.5 0.3 shard_map.99
  21.8 2.6 %collective-permute-done.7.refs_2_ = s16[32,640]{1,0:T(8,128)(2,1)S(1)} collective-permute-done((s16[32,640]{1,0:T(8,128)(2,1)S(1)}, s16[32,640]{1,0:T(8,128)(2,1)S(1)}, u32[]{:S(2)}, u32[]{:S(2)}) %collective-permute-start.7) | collective-permute-done | bytes 40992 | tf_op jit(solution)/shard_map/ppermute | solution.py:283
  24.4 0.3 shard_map.100
  24.7 0.0 collective-permute-start.8
  24.7 1.4 %collective-permute-done.8.refs_1_ = f32[32,1152]{1,0:T(8,128)S(1)} collective-permute-done((f32[32,1152]{1,0:T(8,128)S(1)}, f32[32,1152]{1,0:T(8,128)S(1)}, u32[]{:S(2)}, u32[]{:S(2)}) %collective-permute-start.8) | collective-permute-done | bytes 147488 | tf_op jit(solution)/shard_map/ppermute | solution.py:283
  26.1 0.1 shard_map.101
  26.2 0.5 %collective-permute-start.10 = (bf16[8,1152]{1,0:T(8,128)(2,1)S(1)}, bf16[8,1152]{1,0:T(8,128)(2,1)S(1)}, u32[]{:S(2)}, u32[]{:S(2)}) collective-permute-start(bf16[8,1152]{1,0:T(8,128)(2,1)S(1)} %get-tuple-element.37), channel_id=1, source_target_pairs={{0,16},{8,24},{16,0},{24,8},{1,17},{9,25},{17,1},{25,9},{2,18},{10... | collective-permute-start | bytes 55304 | tf_op jit(solution)/shard_map/ppermute | solution.py:283
  26.7 1.5 %collective-permute-start.11 = (bf16[8,1152]{1,0:T(8,128)(2,1)S(1)}, bf16[8,1152]{1,0:T(8,128)(2,1)S(1)}, u32[]{:S(2)}, u32[]{:S(2)}) collective-permute-start(bf16[8,1152]{1,0:T(8,128)(2,1)S(1)} %get-tuple-element.38), channel_id=1, source_target_pairs={{0,24},{8,16},{16,8},{24,0},{1,25},{9,17},{17,9},{25,1},{2,26},{10... | collective-permute-start | bytes 55304 | tf_op jit(solution)/shard_map/ppermute | solution.py:283
  28.2 1.5 %collective-permute-start.9 = (bf16[8,1152]{1,0:T(8,128)(2,1)S(1)}, bf16[8,1152]{1,0:T(8,128)(2,1)S(1)}, u32[]{:S(2)}, u32[]{:S(2)}) collective-permute-start(bf16[8,1152]{1,0:T(8,128)(2,1)S(1)} %get-tuple-element.36), channel_id=1, source_target_pairs={{0,8},{8,0},{16,24},{24,16},{1,9},{9,1},{17,25},{25,17},{2,10},{10... | collective-permute-start | bytes 55304 | tf_op jit(solution)/shard_map/ppermute | solution.py:283
  29.7 1.6 %shard_map.103 = (f32[1024,256]{1,0:T(8,128)}, f32[256,1024]{1,0:T(8,128)}) custom-call(bf16[64,1152]{1,0:T(8,128)(2,1)S(1)} %shard_map.94.refs_0_, bf16[64,1152]{1,0:T(8,128)(2,1)S(1)} %collective-permute-done.3.refs_1_, bf16[64,256]{1,0:T(8,128)(2,1)S(1)} %get-tuple-element.32.refs_0_.refs_2_, bf16[64,256]{1,0:T(8,128)(2,1)S(1)} %get-tuple-element.43.refs_3_, ...), custom_call_target="tpu_custom_call" | custom-call | flops 134217728 | bytes 2097152 | tf_op jit(solution)/shard_map/pallas_call | solution.py:38
  31.3 0.0 collective-permute-done.10.refs_2_
  31.3 0.0 collective-permute-done.11.refs_3_
  31.4 0.6 %collective-permute-done.9.refs_1_ = bf16[8,1152]{1,0:T(8,128)(2,1)S(1)} collective-permute-done((bf16[8,1152]{1,0:T(8,128)(2,1)S(1)}, bf16[8,1152]{1,0:T(8,128)(2,1)S(1)}, u32[]{:S(2)}, u32[]{:S(2)}) %collective-permute-start.9) | collective-permute-done | bytes 18464 | tf_op jit(solution)/shard_map/ppermute | solution.py:283
  31.9 1.6 %shard_map.102 = (bf16[256,1024]{1,0:T(8,128)(2,1)}, f32[2,256]{1,0:T(2,128)}) custom-call(f32[8,1152]{1,0:T(8,128)S(1)} %get-tuple-element.35.refs_0_, bf16[8,1152]{1,0:T(8,128)(2,1)S(1)} %collective-permute-done.9.refs_1_, bf16[8,1152]{1,0:T(8,128)(2,1)S(1)} %collective-permute-done.10.refs_2_, bf16[8,1152]{1,0:T(8,128)(2,1)S(1)} %collective-permute-done.11.refs_3_, ...), custom_call_target="tpu_custom_call" | custom-call | flops 16777216 | bytes 524288 | tf_op jit(solution)/shard_map/pallas_call | solution.py:38
  (1 shorter events, 0.0 us)
Async XLA Ops:
  0.6 11.2 %copy-start = (bf16[1024,256]{1,0:T(8,128)(2,1)S(1)}, bf16[1024,256]{1,0:T(8,128)(2,1)}, u32[]{:S(2)}) copy-start(bf16[1024,256]{1,0:T(8,128)(2,1)} %refs_4_.3) | copy-start | bytes 1572868
  0.6 11.2 %copy-start.1 = (bf16[256,1024]{1,0:T(8,128)(2,1)S(1)}, bf16[256,1024]{1,0:T(8,128)(2,1)}, u32[]{:S(2)}) copy-start(bf16[256,1024]{1,0:T(8,128)(2,1)} %refs_3_.3) | copy-start | bytes 1572868
  2.4 4.9 %collective-permute-start = (bf16[16,1152]{1,0:T(8,128)(2,1)S(1)}, bf16[16,1152]{1,0:T(8,128)(2,1)S(1)}, u32[]{:S(2)}, u32[]{:S(2)}) collective-permute-start(bf16[16,1152]{1,0:T(8,128)(2,1)S(1)} %get-tuple-element.26.refs_0_), channel_id=1, source_target_pairs={{0,8},{8,0},{16,24},{24,16},{1,9},{9,1},{17,25},{25,17},{2,10},{10... | collective-permute-start | bytes 110600 | tf_op jit(solution)/shard_map/ppermute | solution.py:283
  5.4 4.0 %collective-permute-start.1 = (bf16[16,1152]{1,0:T(8,128)(2,1)S(1)}, bf16[16,1152]{1,0:T(8,128)(2,1)S(1)}, u32[]{:S(2)}, u32[]{:S(2)}) collective-permute-start(bf16[16,1152]{1,0:T(8,128)(2,1)S(1)} %get-tuple-element.27), channel_id=1, source_target_pairs={{0,16},{8,24},{16,0},{24,8},{1,17},{9,25},{17,1},{25,9},{2,18},{10... | collective-permute-start | bytes 110600 | tf_op jit(solution)/shard_map/ppermute | solution.py:283
  6.9 4.9 %collective-permute-start.2 = (bf16[16,1152]{1,0:T(8,128)(2,1)S(1)}, bf16[16,1152]{1,0:T(8,128)(2,1)S(1)}, u32[]{:S(2)}, u32[]{:S(2)}) collective-permute-start(bf16[16,1152]{1,0:T(8,128)(2,1)S(1)} %get-tuple-element.27), channel_id=1, source_target_pairs={{0,24},{8,16},{16,8},{24,0},{1,25},{9,17},{17,9},{25,1},{2,26},{10... | collective-permute-start | bytes 110600 | tf_op jit(solution)/shard_map/ppermute | solution.py:283
  11.7 2.2 %collective-permute-start.3 = (bf16[64,1152]{1,0:T(8,128)(2,1)S(1)}, bf16[64,1152]{1,0:T(8,128)(2,1)S(1)}, u32[]{:S(2)}, u32[]{:S(2)}) collective-permute-start(bf16[64,1152]{1,0:T(8,128)(2,1)S(1)} %shard_map.94.refs_0_), channel_id=1, source_target_pairs={{0,4},{4,0},{1,5},{5,1},{2,6},{6,2},{3,7},{7,3},{8,12},{12,8},{9,1... | collective-permute-start | bytes 442376 | tf_op jit(solution)/shard_map/ppermute | solution.py:283
  12.3 4.1 %collective-permute-start.4 = (s16[32,640]{1,0:T(8,128)(2,1)S(1)}, s16[32,640]{1,0:T(8,128)(2,1)S(1)}, u32[]{:S(2)}, u32[]{:S(2)}) collective-permute-start(s16[32,640]{1,0:T(8,128)(2,1)S(1)} %get-tuple-element.28.refs_0_.refs_1_), channel_id=1, source_target_pairs={{0,1},{1,0},{2,3},{3,2},{4,5},{5,4},{6,7},{7,6},{8,9},{9,8},{10,11... | collective-permute-start | bytes 122888 | tf_op jit(solution)/shard_map/ppermute | solution.py:283
  14.4 4.8 %collective-permute-start.5 = (s16[32,640]{1,0:T(8,128)(2,1)S(1)}, s16[32,640]{1,0:T(8,128)(2,1)S(1)}, u32[]{:S(2)}, u32[]{:S(2)}) collective-permute-start(s16[32,640]{1,0:T(8,128)(2,1)S(1)} %get-tuple-element.29.refs_0_.refs_1_), channel_id=1, source_target_pairs={{0,1},{1,0},{2,3},{3,2},{4,5},{5,4},{6,7},{7,6},{8,9},{9,8},{10,11... | collective-permute-start | bytes 122888 | tf_op jit(solution)/shard_map/ppermute | solution.py:283
  16.6 5.0 %collective-permute-start.6 = (s16[32,640]{1,0:T(8,128)(2,1)S(1)}, s16[32,640]{1,0:T(8,128)(2,1)S(1)}, u32[]{:S(2)}, u32[]{:S(2)}) collective-permute-start(s16[32,640]{1,0:T(8,128)(2,1)S(1)} %shard_map.97.refs_0_.refs_1_), channel_id=1, source_target_pairs={{0,2},{1,3},{2,0},{3,1},{4,6},{5,7},{6,4},{7,5},{8,10},{9,11},{10,... | collective-permute-start | bytes 122888 | tf_op jit(solution)/shard_map/ppermute | solution.py:283
  19.4 5.0 %collective-permute-start.7 = (s16[32,640]{1,0:T(8,128)(2,1)S(1)}, s16[32,640]{1,0:T(8,128)(2,1)S(1)}, u32[]{:S(2)}, u32[]{:S(2)}) collective-permute-start(s16[32,640]{1,0:T(8,128)(2,1)S(1)} %shard_map.98.refs_0_.refs_1_), channel_id=1, source_target_pairs={{0,2},{1,3},{2,0},{3,1},{4,6},{5,7},{6,4},{7,5},{8,10},{9,11},{10,... | collective-permute-start | bytes 122888 | tf_op jit(solution)/shard_map/ppermute | solution.py:283
  24.7 1.4 %collective-permute-start.8 = (f32[32,1152]{1,0:T(8,128)S(1)}, f32[32,1152]{1,0:T(8,128)S(1)}, u32[]{:S(2)}, u32[]{:S(2)}) collective-permute-start(f32[32,1152]{1,0:T(8,128)S(1)} %get-tuple-element.34), channel_id=1, source_target_pairs={{0,4},{4,0},{1,5},{5,1},{2,6},{6,2},{3,7},{7,3},{8,12},{12,8},{9,1... | collective-permute-start | bytes 442376 | tf_op jit(solution)/shard_map/ppermute | solution.py:283
  26.2 5.2 %collective-permute-start.10 = (bf16[8,1152]{1,0:T(8,128)(2,1)S(1)}, bf16[8,1152]{1,0:T(8,128)(2,1)S(1)}, u32[]{:S(2)}, u32[]{:S(2)}) collective-permute-start(bf16[8,1152]{1,0:T(8,128)(2,1)S(1)} %get-tuple-element.37), channel_id=1, source_target_pairs={{0,16},{8,24},{16,0},{24,8},{1,17},{9,25},{17,1},{25,9},{2,18},{10... | collective-permute-start | bytes 55304 | tf_op jit(solution)/shard_map/ppermute | solution.py:283
  26.7 4.7 %collective-permute-start.11 = (bf16[8,1152]{1,0:T(8,128)(2,1)S(1)}, bf16[8,1152]{1,0:T(8,128)(2,1)S(1)}, u32[]{:S(2)}, u32[]{:S(2)}) collective-permute-start(bf16[8,1152]{1,0:T(8,128)(2,1)S(1)} %get-tuple-element.38), channel_id=1, source_target_pairs={{0,24},{8,16},{16,8},{24,0},{1,25},{9,17},{17,9},{25,1},{2,26},{10... | collective-permute-start | bytes 55304 | tf_op jit(solution)/shard_map/ppermute | solution.py:283
  28.2 3.8 %collective-permute-start.9 = (bf16[8,1152]{1,0:T(8,128)(2,1)S(1)}, bf16[8,1152]{1,0:T(8,128)(2,1)S(1)}, u32[]{:S(2)}, u32[]{:S(2)}) collective-permute-start(bf16[8,1152]{1,0:T(8,128)(2,1)S(1)} %get-tuple-element.36), channel_id=1, source_target_pairs={{0,8},{8,0},{16,24},{24,16},{1,9},{9,1},{17,25},{25,17},{2,10},{10... | collective-permute-start | bytes 55304 | tf_op jit(solution)/shard_map/ppermute | solution.py:283

commit v2 on v1

--- a/solution.py
+++ b/solution.py
@@ -156,17 +156,25 @@
         out_ref[index * rows : (index + 1) * rows] = ref[...]
 
 
-def part_kernel(capacity, rows_ref, w_in_ref, w_out_ref, part_ref, gate_ref):
+def part_kernel(capacity, rows_ref, w_in_ref, w_in_other_ref, w_out_ref, w_out_other_ref, part_ref,
+                gate_ref):
     feats, hidden = w_in_ref.shape
     groups = rows_ref.shape[0] // (2 * capacity)
     gate = rows_ref[:, feats:].astype(F32).reshape(groups, 2 * capacity, LANES)
     gate_ref[...] = gate[:, :capacity].reshape(groups * capacity, LANES)
     rows = rows_ref[:, :feats]
-    pre = jnp.dot(rows, w_in_ref[...], preferred_element_type=F32)
-    back = lax.dot_general(rows, w_out_ref[...], COLS_BY_COLS, preferred_element_type=F32)
-    pre = pre.reshape(groups, 2 * capacity, hidden)[:, :capacity]
-    back = back.reshape(groups, 2 * capacity, hidden)[:, capacity:]
-    store_codes(part_ref, [value.reshape(groups * capacity, hidden) for value in (pre, back)])
+    pre = [
+        jnp.dot(rows, ref[...], preferred_element_type=F32) for ref in (w_in_ref, w_in_other_ref)
+    ]
+    back = [
+        lax.dot_general(rows, ref[...], COLS_BY_COLS, preferred_element_type=F32)
+        for ref in (w_out_ref, w_out_other_ref)
+    ]
+    pair = []
+    for values, span in ((pre, slice(0, capacity)), (back, slice(capacity, 2 * capacity))):
+        values = jnp.concatenate(values, axis=1).reshape(groups, 2 * capacity, 2 * hidden)
+        pair.append(values[:, span].reshape(groups * capacity, 2 * hidden))
+    store_codes(part_ref, pair)
 
 
 def add_codes_kernel(first_ref, second_ref, out_ref):
@@ -174,25 +182,44 @@
     store_codes(out_ref, [first + second for first, second in pairs])
 
 
-def slot_kernel(capacity, first_ref, second_ref, gate_ref, w_in_ref, slot_ref, dpre_ref, act_ref):
-    feats, hidden = w_in_ref.shape
+def deal(total, keep_ref, send_refs):
+    each, wide = keep_ref.shape
+    feats = wide - LANES
+    keep_ref[...] = total[:each]
+    gate = split_value(jnp.sum(total[:, feats:], axis=1, keepdims=True))
+    for index, send_ref in enumerate(send_refs):
+        span = slice((index + 1) * each, (index + 2) * each)
+        send_ref[:, :feats] = total[span, :feats].astype(BF16)
+        send_ref[:, feats:] = gate[span].astype(BF16)
+
+
+def slot_kernel(capacity, first_ref, second_ref, gate_ref, w_in_ref, w_in_other_ref, mine_ref,
+                theirs_ref, *slot_refs):
+    hidden = w_in_ref.shape[1]
     pairs = zip(load_codes(first_ref), load_codes(second_ref))
     pre, back = [first + second for first, second in pairs]
     gate = gate_ref[:, :1]
     activation, slopes = gelu_pair(pre)
     dpre = (gate * back * slopes).astype(BF16)
     act = gate * activation
+    slot = lax.dot_general(
+        dpre[:, :hidden], w_in_ref[...], COLS_BY_COLS, preferred_element_type=F32
+    ) + lax.dot_general(
+        dpre[:, hidden:], w_in_other_ref[...], COLS_BY_COLS, preferred_element_type=F32
+    )
+    slot_gate = split_value(jnp.sum(activation * back, axis=1, keepdims=True))
+    total = jnp.concatenate([slot, slot_gate], axis=1)
+    if len(slot_refs) == 1:
+        slot_refs[0][...] = total
+    else:
+        deal(total, slot_refs[0], slot_refs[1:])
     rows = dpre.shape[0]
-    slot_ref[:, :feats] = lax.dot_general(
-        dpre, w_in_ref[...], COLS_BY_COLS, preferred_element_type=F32
-    )
-    slot_ref[:, feats:] = split_value(jnp.sum(activation * back, axis=1, keepdims=True))
-    groups = rows // capacity
-    dpre = dpre.astype(F32).reshape(groups, capacity, hidden)
-    act = act.reshape(groups, capacity, hidden)
-    blank = jnp.zeros_like(dpre)
-    dpre_ref[...] = jnp.concatenate([dpre, blank], axis=1).reshape(2 * rows, hidden).astype(BF16)
-    act_ref[...] = jnp.concatenate([blank, act], axis=1).reshape(2 * rows, hidden).astype(BF16)
+    both = [
+        value.reshape(rows // capacity, capacity, 2 * hidden) for value in (dpre.astype(F32), act)
+    ]
+    both = jnp.concatenate(both, axis=1).reshape(2 * rows, 2 * hidden).astype(BF16)
+    mine_ref[...] = both[:, :hidden]
+    theirs_ref[...] = both[:, hidden:]
 
 
 def halve_kernel(kept_ref, came_ref, keep_ref, send_ref):
@@ -203,23 +230,17 @@
 
 
 def deal_kernel(kept_ref, came_ref, keep_ref, *send_refs):
-    each, wide = keep_ref.shape
-    feats = wide - LANES
-    total = kept_ref[...] + came_ref[...]
-    keep_ref[...] = total[:each]
-    gate = split_value(jnp.sum(total[:, feats:], axis=1, keepdims=True))
-    for index, send_ref in enumerate(send_refs):
-        span = slice((index + 1) * each, (index + 2) * each)
-        send_ref[:, :feats] = total[span, :feats].astype(BF16)
-        send_ref[:, feats:] = gate[span].astype(BF16)
-
-
-def weight_kernel(held_ref, came_ref, dpre_held_ref, dpre_came_ref, act_held_ref, act_came_ref,
-                  w_in_hbm, w_out_hbm, w_in_ref, w_out_ref, sems):
+    deal(kept_ref[...] + came_ref[...], keep_ref, send_refs)
+
+
+def weight_kernel(capacity, held_ref, came_ref, mine_ref, back_ref, w_in_hbm, w_out_hbm,
+                  written_ref, w_in_ref, w_out_ref, sems):
     feats, hidden = w_in_ref.shape
     rows = jnp.concatenate([held_ref[:, :feats], came_ref[:, :feats]], axis=0)
-    dpre = jnp.concatenate([dpre_held_ref[...], dpre_came_ref[...]], axis=0)
-    act = jnp.concatenate([act_held_ref[...], act_came_ref[...]], axis=0)
+    both = jnp.concatenate([mine_ref[...], back_ref[...]], axis=0).astype(F32)
+    of_x = lax.broadcasted_iota(jnp.int32, both.shape, 0) % (2 * capacity) < capacity
+    dpre = jnp.where(of_x, both, 0.0).astype(BF16)
+    act = jnp.where(of_x, 0.0, both).astype(BF16)
     count = feats // PIECES
     copies = []
     for piece in range(PIECES):
@@ -237,11 +258,12 @@
             copies.append(copy)
     for copy in copies:
         copy.wait()
+    written_ref[...] = jnp.zeros(written_ref.shape, F32)
 
 
 def combine_kernel(steps, *refs):
     kept_ref, came_refs = refs[0], refs[1:steps]
-    place_ref, spread_ref, tokens_hbm, gate_out_ref, tokens_ref, sems = refs[steps:]
+    place_ref, spread_ref, tokens_ref, gate_out_ref = refs[steps:]
     feats = tokens_ref.shape[1]
     capacity = kept_ref.shape[0]
     came = [ref[...].astype(F32) for ref in came_refs]
@@ -253,18 +275,7 @@
     high = grads.astype(BF16)
     low = (grads - high.astype(F32)).astype(BF16)
     both = jnp.concatenate([high, low], axis=0)
-    spread = spread_ref[...]
-    count = feats // PIECES
-    copies = []
-    for piece in range(PIECES):
-        span = slice(piece * count, (piece + 1) * count)
-        tokens_ref[:, span] = jnp.dot(
-            spread, both[:, span], preferred_element_type=F32
-        ).astype(BF16)
-        span = pl.ds(piece * count, count)
-        copy = pltpu.make_async_copy(tokens_ref.at[:, span], tokens_hbm.at[:, span], sems.at[piece])
-        copy.start()
-        copies.append(copy)
+    tokens_ref[...] = jnp.dot(spread_ref[...], both, preferred_element_type=F32).astype(BF16)
     slot_gate = jnp.sum(slots[:, feats:], axis=1, keepdims=True)
     picked = place_ref[: WINDOW * capacity].astype(F32) * slot_gate
     masks = place_ref[WINDOW * capacity :].astype(F32)
@@ -274,8 +285,6 @@
         value = jnp.sum(picked[span], axis=0, keepdims=True)
         result = result + masks[2 * index : 2 * index + 2] * value
     gate_out_ref[...] = result
-    for copy in copies:
-        copy.wait()
 
 
 def swap(array, axes, bit):
@@ -297,9 +306,9 @@
     hidden = w_in.shape[1]
     capacity = 2 * tok_rows // EXPERTS
     slots = WINDOW * capacity
-    rows = nodes * locals_ * capacity
+    rows = nodes * (locals_ // 2) * capacity
     wide = feats + LANES
-    coded = 2 * hidden + LANES
+    coded = 4 * hidden + LANES
     shape = jax.ShapeDtypeStruct
     hbm = pl.BlockSpec(memory_space=pltpu.HBM)
     vmem = pl.BlockSpec(memory_space=pltpu.VMEM)
@@ -328,104 +337,77 @@
         ],
     )(routes_t, gates_t, tokens, grad_out)
 
+    w_in_other, w_out_other = swap(w_in, "local", 1), swap(w_out, "local", 1)
+
     pieces = [own_rows] * nodes
     for step in reversed(range(1, nodes)):
         pieces[step] = swap(own_rows if step < nodes // WINDOW else other_rows, "node", step)
     held = join(pieces)
-    came = swap(held, "local", 1)
     bit = 2
     while bit < locals_:
-        held = join([held, came])
-        came = swap(held, "local", bit)
+        held = join([held, swap(held, "local", bit)])
         bit *= 2
-
-    half = rows // 2
-    last = ()
-    sums = []
-    for chunk in (held, came):
-        part, gate_rows = call(
-            functools.partial(part_kernel, capacity),
-            (shape((half, coded), I16), shape((half, LANES), F32)),
-            8 * half * feats * hidden,
-            4 * half * feats + 4 * feats * hidden,
-            after=last,
-        )(chunk, w_in, w_out)
-        last = (part,)
-        sums.append([part, swap(part, "edata", 1), gate_rows])
-    bit = 2
-    while bit < edatas:
-        for index, (part, other, gate_rows) in enumerate(sums):
-            part = call(
-                add_codes_kernel,
-                shape((half, coded), I16),
-                8 * half * hidden,
-                6 * half * coded,
-                after=last,
-            )(part, other)
-            last = (part,)
-            sums[index] = [part, swap(part, "edata", bit), gate_rows]
+    came = swap(held, "local", 1)
+
+    part, gate_rows = call(
+        functools.partial(part_kernel, capacity),
+        (shape((rows, coded), I16), shape((rows, LANES), F32)),
+        16 * rows * feats * hidden,
+        4 * rows * feats + 8 * feats * hidden,
+    )(held, w_in, w_in_other, w_out, w_out_other)
+    bit = 1
+    other = swap(part, "edata", bit)
+    while 2 * bit < edatas:
+        part = call(
+            add_codes_kernel, shape((rows, coded), I16), 16 * rows * hidden, 6 * rows * coded
+        )(part, other)
         bit *= 2
-    slot_parts = []
-    operands = []
-    for part, other, gate_rows in sums:
-        slot, dpre, act = call(
-            functools.partial(slot_kernel, capacity),
-            (
-                shape((half, wide), F32),
-                shape((2 * half, hidden), BF16),
-                shape((2 * half, hidden), BF16),
-            ),
-            2 * half * feats * hidden,
-            2 * feats * hidden + 4 * half * feats,
-            after=last,
-        )(part, other, gate_rows, w_in)
-        last = (dpre,)
-        slot_parts.append(slot)
-        operands.append((dpre, act))
-
-    keep, send = slot_parts
-    back = swap(send, "local", locals_ // 2)
-    bit = locals_ // 4
-    while bit:
-        half //= 2
-        keep, send = call(
-            halve_kernel, (shape((half, wide), F32),) * 2, 4 * half * wide, 24 * half * wide
-        )(keep, back)
-        back = swap(send, "local", bit)
-        bit //= 2
-    keep, *sends = call(
-        deal_kernel,
-        (shape((capacity, wide), F32),) + (shape((capacity, wide), BF16),) * (nodes - 1),
-        4 * half * wide,
-        12 * half * wide,
-    )(keep, back)
-    backs = [swap(send, "node", step + 1) for step, send in reversed(list(enumerate(sends)))]
-    (dpre_held, act_held), (dpre_came, act_came) = operands
-    grad_w_in, grad_w_out = call(
-        weight_kernel,
-        (shape((feats, hidden), F32), shape((hidden, feats), F32)),
-        8 * rows * feats * hidden,
+        other = swap(part, "edata", bit)
+
+    dealt = (shape((capacity, wide), F32),) + (shape((capacity, wide), BF16),) * (nodes - 1)
+    mine, theirs, *slot_parts = call(
+        functools.partial(slot_kernel, capacity),
+        (shape((2 * rows, hidden), BF16),) * 2
+        + (dealt if locals_ == 2 else (shape((rows, wide), F32),)),
+        4 * rows * feats * hidden,
+        4 * feats * hidden + 4 * rows * feats,
+    )(part, other, gate_rows, w_in, w_in_other)
+    back = swap(theirs, "local", 1)
+    if locals_ > 2:
+        half = rows // 2
+        keep, send = slot_parts[0][:half], slot_parts[0][half:]
+        bit = locals_ // 2
+        while bit > 2:
+            half //= 2
+            keep, send = call(
+                halve_kernel, (shape((half, wide), F32),) * 2, 4 * half * wide, 24 * half * wide
+            )(keep, swap(send, "local", bit))
+            bit //= 2
+        slot_parts = call(deal_kernel, dealt, 4 * half * wide, 12 * half * wide)(
+            keep, swap(send, "local", bit)
+        )
+    keep, *sends = slot_parts
+    backs = [swap(send, "node", step + 1) for step, send in enumerate(sends)]
+    grad_w_in, grad_w_out, written = call(
+        functools.partial(weight_kernel, capacity),
+        (shape((feats, hidden), F32), shape((hidden, feats), F32), shape((8, LANES), F32)),
+        16 * rows * feats * hidden,
         8 * feats * hidden,
-        in_specs=[vmem] * 6,
-        out_specs=[hbm] * 2,
+        in_specs=[vmem] * 4,
+        out_specs=[hbm, hbm, vmem],
         scratch_shapes=[
             pltpu.VMEM((feats, hidden), F32),
             pltpu.VMEM((hidden, feats), F32),
             pltpu.SemaphoreType.DMA((2 * PIECES,)),
         ],
-    )(held, came, dpre_held, dpre_came, act_held, act_came)
+    )(held, came, mine, back)
     grad_tokens, grad_gates = call(
         functools.partial(combine_kernel, nodes),
         (shape((tok_rows, feats), BF16), shape((2, tok_rows), F32)),
         4 * slots * tok_rows * feats,
         2 * tok_rows * feats,
-        in_specs=[vmem] * (nodes + 2),
-        out_specs=[hbm, vmem],
-        scratch_shapes=[
-            pltpu.VMEM((tok_rows, feats), BF16),
-            pltpu.SemaphoreType.DMA((PIECES,)),
-        ],
-    )(keep, *reversed(backs), place, spread)
+        after=(written,),
+    )(keep, *backs, place, spread)
     return (grad_tokens, grad_gates.T, grad_w_in, grad_w_out)
 
 

time: 33.7 us -> 30.5 us (0.905)
  starting transfers between devices: 15.4 us -> 13 us
  Pallas kernels: 6.86 us -> 5.78 us
    ppermute x12, starting transfers between devices: 15.4 us -> 13 us  [swap(): lax.ppermute(array, axes, [(index, index ^ bit) for index in range(size)])]
    pallas_call x11 -> x7, Pallas kernels: 6.86 us -> 5.78 us  [run(): pl.pallas_call(lambda *refs: kernel(*refs[len(after):]), out_shape=out_sh...]
  transfers between devices with their start and end apart: 12 -> 12, of which waited for: 8 -> 7; matrix products, arithmetic and copies ran while one was open for 0% -> 0% of each run, Pallas kernels for 10% -> 13%
where the time goes in v2:
time: 30.5 us; the launch traced here: 30.4 us
  starting transfers between devices  13 us (43%)
  waiting for transfers between devices  10.9 us (36%)
  Pallas kernels  5.78 us (19%)
  between operations  0.72 us (2%)
    ppermute x12, starting transfers between devices, swap(): lax.ppermute(array, axes, [(index, index ^ bit) for index in range(size)])  13 us
    ppermute x12, waiting for transfers between devices, swap(): lax.ppermute(array, axes, [(index, index ^ bit) for index in range(size)])  10.9 us
    pallas_call x7, Pallas kernels, run(): pl.pallas_call(lambda *refs: kernel(*refs[len(after):]), out_shape=out_sh...  5.78 us
  transfers between devices with their start and end apart: 12, of which 7 were waited for; matrix products, arithmetic and copies ran while one was open for 0% of the time, Pallas kernels for 13%

profile of v2, /device:TPU:0, one launch (start us, length us, event | category | flops | bytes accessed | tf_op | source)
XLA Modules:
  0.0 30.4 jit_solution(7810114190446814468)
XLA Ops:
  0.6 0.5 %collective-permute-start.5 = (bf16[256,1024]{1,0:T(8,128)(2,1)}, bf16[256,1024]{1,0:T(8,128)(2,1)S(1)}, u32[]{:S(2)}, u32[]{:S(2)}) collective-permute-start(bf16[256,1024]{1,0:T(8,128)(2,1)} %refs_3_.4), channel_id=1, source_target_pairs={{0,4},{4,0},{1,5},{5,1},{2,6},{6,2},{3,7},{7,3},{8,12},{12,8},{9,1... | collective-permute-start | bytes 1572872 | tf_op jit(solution)/shard_map/ppermute | solution.py:292
  1.2 0.1 collective-permute-start.4
  1.2 0.0 copy-start
  1.2 0.0 copy-start.1
  1.2 1.7 %shard_map.93 = (bf16[16,1152]{1,0:T(8,128)(2,1)S(1)}, bf16[16,1152]{1,0:T(8,128)(2,1)S(1)}, bf16[32,256]{1,0:T(8,128)(2,1)S(1)}, bf16[256,32]{1,0:T(8,128)(2,1)S(1)}) custom-call(s32[2,256]{1,0:T(2,128)} %bitcast.3, bf16[2,256]{1,0:T(2,128)(2,1)} %bitcast.4, bf16[256,1024]{1,0:T(8,128)(2,1)} %refs_2_.1, bf16[256,1024]{1,0:T(8,128)(2,1)} %refs_3_.3), custom_call_target="tpu_custom_call" | custom-call | flops 16777216 | bytes 1048576 | tf_op jit(solution)/shard_map/pallas_call | solution.py:38
  2.9 3.0 %collective-permute-start = (bf16[16,1152]{1,0:T(8,128)(2,1)S(1)}, bf16[16,1152]{1,0:T(8,128)(2,1)S(1)}, u32[]{:S(2)}, u32[]{:S(2)}) collective-permute-start(bf16[16,1152]{1,0:T(8,128)(2,1)S(1)} %get-tuple-element.21.refs_0_), channel_id=1, source_target_pairs={{0,8},{8,0},{16,24},{24,16},{1,9},{9,1},{17,25},{25,17},{2,10},{10... | collective-permute-start | bytes 110600 | tf_op jit(solution)/shard_map/ppermute | solution.py:292
  5.9 1.5 %collective-permute-start.2 = (bf16[16,1152]{1,0:T(8,128)(2,1)S(1)}, bf16[16,1152]{1,0:T(8,128)(2,1)S(1)}, u32[]{:S(2)}, u32[]{:S(2)}) collective-permute-start(bf16[16,1152]{1,0:T(8,128)(2,1)S(1)} %get-tuple-element.22), channel_id=1, source_target_pairs={{0,24},{8,16},{16,8},{24,0},{1,25},{9,17},{17,9},{25,1},{2,26},{10... | collective-permute-start | bytes 110600 | tf_op jit(solution)/shard_map/ppermute | solution.py:292
  7.4 0.1 collective-permute-start.1
  7.5 0.4 %collective-permute-done.refs_1_ = bf16[16,1152]{1,0:T(8,128)(2,1)S(1)} collective-permute-done((bf16[16,1152]{1,0:T(8,128)(2,1)S(1)}, bf16[16,1152]{1,0:T(8,128)(2,1)S(1)}, u32[]{:S(2)}, u32[]{:S(2)}) %collective-permute-start) | collective-permute-done | bytes 36896 | tf_op jit(solution)/shard_map/ppermute | solution.py:292
  7.9 2.9 %collective-permute-done.2.refs_3_ = bf16[16,1152]{1,0:T(8,128)(2,1)S(1)} collective-permute-done((bf16[16,1152]{1,0:T(8,128)(2,1)S(1)}, bf16[16,1152]{1,0:T(8,128)(2,1)S(1)}, u32[]{:S(2)}, u32[]{:S(2)}) %collective-permute-start.2) | collective-permute-done | bytes 36896 | tf_op jit(solution)/shard_map/ppermute | solution.py:292
  10.8 0.6 %collective-permute-done.1.refs_2_ = bf16[16,1152]{1,0:T(8,128)(2,1)S(1)} collective-permute-done((bf16[16,1152]{1,0:T(8,128)(2,1)S(1)}, bf16[16,1152]{1,0:T(8,128)(2,1)S(1)}, u32[]{:S(2)}, u32[]{:S(2)}) %collective-permute-start.1) | collective-permute-done | bytes 36896 | tf_op jit(solution)/shard_map/ppermute | solution.py:292
  11.4 0.0 collective-permute-done.5.refs_4_
  11.4 0.0 collective-permute-done.4.refs_2_.refs_4_
  11.4 0.0 copy-done
  11.4 0.0 copy-done.1
  11.4 0.7 %shard_map.95 = (s16[32,1152]{1,0:T(8,128)(2,1)S(1)}, f32[32,128]{1,0:T(8,128)S(1)}) custom-call(bf16[64,1152]{1,0:T(8,128)(2,1)S(1)} %shard_map.94.refs_0_, bf16[1024,256]{1,0:T(8,128)(2,1)S(1)} %copy-done, bf16[1024,256]{1,0:T(8,128)(2,1)S(1)} %collective-permute-done.4.refs_2_.refs_4_, bf16[256,1024]{1,0:T(8,128)(2,1)S(1)} %copy-done.1, ...), custom_call_target="tpu_custom_call" | custom-call | flops 134217728 | bytes 2228224 | tf_op jit(solution)/shard_map/pallas_call | solution.py:38
  12.2 1.6 %collective-permute-start.6 = (s16[32,1152]{1,0:T(8,128)(2,1)S(1)}, s16[32,1152]{1,0:T(8,128)(2,1)S(1)}, u32[]{:S(2)}, u32[]{:S(2)}) collective-permute-start(s16[32,1152]{1,0:T(8,128)(2,1)S(1)} %get-tuple-element.23.refs_0_), channel_id=1, source_target_pairs={{0,1},{1,0},{2,3},{3,2},{4,5},{5,4},{6,7},{7,6},{8,9},{9,8},{10,11... | collective-permute-start | bytes 221192 | tf_op jit(solution)/shard_map/ppermute | solution.py:292
  13.8 0.0 collective-permute-start.3
  13.8 2.8 %collective-permute-done.6.refs_1_ = s16[32,1152]{1,0:T(8,128)(2,1)S(1)} collective-permute-done((s16[32,1152]{1,0:T(8,128)(2,1)S(1)}, s16[32,1152]{1,0:T(8,128)(2,1)S(1)}, u32[]{:S(2)}, u32[]{:S(2)}) %collective-permute-start.6) | collective-permute-done | bytes 73760 | tf_op jit(solution)/shard_map/ppermute | solution.py:292
  16.6 0.2 shard_map.96.refs_0_
  16.8 2.7 %collective-permute-start.7 = (s16[32,1152]{1,0:T(8,128)(2,1)S(1)}, s16[32,1152]{1,0:T(8,128)(2,1)S(1)}, u32[]{:S(2)}, u32[]{:S(2)}) collective-permute-start(s16[32,1152]{1,0:T(8,128)(2,1)S(1)} %shard_map.96.refs_0_), channel_id=1, source_target_pairs={{0,2},{1,3},{2,0},{3,1},{4,6},{5,7},{6,4},{7,5},{8,10},{9,11},{10,... | collective-permute-start | bytes 221192 | tf_op jit(solution)/shard_map/ppermute | solution.py:292
  19.4 2.7 %collective-permute-done.7.refs_1_ = s16[32,1152]{1,0:T(8,128)(2,1)S(1)} collective-permute-done((s16[32,1152]{1,0:T(8,128)(2,1)S(1)}, s16[32,1152]{1,0:T(8,128)(2,1)S(1)}, u32[]{:S(2)}, u32[]{:S(2)}) %collective-permute-start.7) | collective-permute-done | bytes 73760 | tf_op jit(solution)/shard_map/ppermute | solution.py:292
  22.1 0.4 %shard_map.97 = (bf16[64,256]{1,0:T(8,128)(2,1)S(1)}, bf16[64,256]{1,0:T(8,128)(2,1)S(1)}, f32[8,1152]{1,0:T(8,128)S(1)}, bf16[8,1152]{1,0:T(8,128)(2,1)S(1)}, b...) custom-call(s16[32,1152]{1,0:T(8,128)(2,1)S(1)} %shard_map.96.refs_0_, ...), custom_call_target="tpu_custom_call" | custom-call | flops 33554432 | bytes 1179648 | tf_op jit(solution)/shard_map/pallas_call | solution.py:38
  22.5 0.1 collective-permute-start.8
  22.6 1.6 %collective-permute-start.9 = (bf16[8,1152]{1,0:T(8,128)(2,1)S(1)}, bf16[8,1152]{1,0:T(8,128)(2,1)S(1)}, u32[]{:S(2)}, u32[]{:S(2)}) collective-permute-start(bf16[8,1152]{1,0:T(8,128)(2,1)S(1)} %get-tuple-element.29), channel_id=1, source_target_pairs={{0,8},{8,0},{16,24},{24,16},{1,9},{9,1},{17,25},{25,17},{2,10},{10... | collective-permute-start | bytes 55304 | tf_op jit(solution)/shard_map/ppermute | solution.py:292
  24.2 0.5 %collective-permute-start.10 = (bf16[8,1152]{1,0:T(8,128)(2,1)S(1)}, bf16[8,1152]{1,0:T(8,128)(2,1)S(1)}, u32[]{:S(2)}, u32[]{:S(2)}) collective-permute-start(bf16[8,1152]{1,0:T(8,128)(2,1)S(1)} %get-tuple-element.30), channel_id=1, source_target_pairs={{0,16},{8,24},{16,0},{24,8},{1,17},{9,25},{17,1},{25,9},{2,18},{10... | collective-permute-start | bytes 55304 | tf_op jit(solution)/shard_map/ppermute | solution.py:292
  24.7 1.5 %collective-permute-start.11 = (bf16[8,1152]{1,0:T(8,128)(2,1)S(1)}, bf16[8,1152]{1,0:T(8,128)(2,1)S(1)}, u32[]{:S(2)}, u32[]{:S(2)}) collective-permute-start(bf16[8,1152]{1,0:T(8,128)(2,1)S(1)} %get-tuple-element.31), channel_id=1, source_target_pairs={{0,24},{8,16},{16,8},{24,0},{1,25},{9,17},{17,9},{25,1},{2,26},{10... | collective-permute-start | bytes 55304 | tf_op jit(solution)/shard_map/ppermute | solution.py:292
  26.2 0.0 collective-permute-done.3.refs_1_
  26.2 0.0 collective-permute-done.8.refs_3_
  26.2 1.6 %shard_map.98 = (f32[1024,256]{1,0:T(8,128)}, f32[256,1024]{1,0:T(8,128)}, f32[8,128]{1,0:T(8,128)S(1)}) custom-call(bf16[64,1152]{1,0:T(8,128)(2,1)S(1)} %shard_map.94.refs_0_, bf16[64,1152]{1,0:T(8,128)(2,1)S(1)} %collective-permute-done.3.refs_1_, bf16[64,256]{1,0:T(8,128)(2,1)S(1)} %get-tuple-element.25.refs_2_, ...), custom_call_target="tpu_custom_call" | custom-call | flops 134217728 | bytes 2097152 | tf_op jit(solution)/shard_map/pallas_call | solution.py:38
  27.8 0.0 collective-permute-done.9.refs_2_
  27.8 0.1 collective-permute-done.10.refs_3_
  27.9 1.4 %collective-permute-done.11.refs_4_ = bf16[8,1152]{1,0:T(8,128)(2,1)S(1)} collective-permute-done((bf16[8,1152]{1,0:T(8,128)(2,1)S(1)}, bf16[8,1152]{1,0:T(8,128)(2,1)S(1)}, u32[]{:S(2)}, u32[]{:S(2)}) %collective-permute-start.11) | collective-permute-done | bytes 18464 | tf_op jit(solution)/shard_map/ppermute | solution.py:292
  29.3 1.1 %shard_map.99 = (bf16[256,1024]{1,0:T(8,128)(2,1)}, f32[2,256]{1,0:T(2,128)}) custom-call(f32[8,128]{1,0:T(8,128)S(1)} %get-tuple-element.27.refs_0_, f32[8,1152]{1,0:T(8,128)S(1)} %get-tuple-element.28.refs_1_, bf16[8,1152]{1,0:T(8,128)(2,1)S(1)} %collective-permute-done.9.refs_2_, bf16[8,1152]{1,0:T(8,128)(2,1)S(1)} %collective-permute-done.10.refs_3_, ...), custom_call_target="tpu_custom_call" | custom-call | flops 16777216 | bytes 524288 | tf_op jit(solution)/shard_map/pallas_call | solution.py:38
  (1 shorter events, 0.0 us)
Async XLA Ops:
  0.6 10.8 %collective-permute-start.5 = (bf16[256,1024]{1,0:T(8,128)(2,1)}, bf16[256,1024]{1,0:T(8,128)(2,1)S(1)}, u32[]{:S(2)}, u32[]{:S(2)}) collective-permute-start(bf16[256,1024]{1,0:T(8,128)(2,1)} %refs_3_.4), channel_id=1, source_target_pairs={{0,4},{4,0},{1,5},{5,1},{2,6},{6,2},{3,7},{7,3},{8,12},{12,8},{9,1... | collective-permute-start | bytes 1572872 | tf_op jit(solution)/shard_map/ppermute | solution.py:292
  1.2 10.2 %collective-permute-start.4 = (bf16[1024,256]{1,0:T(8,128)(2,1)}, bf16[1024,256]{1,0:T(8,128)(2,1)S(1)}, u32[]{:S(2)}, u32[]{:S(2)}) collective-permute-start(bf16[1024,256]{1,0:T(8,128)(2,1)} %refs_3_.5), channel_id=1, source_target_pairs={{0,4},{4,0},{1,5},{5,1},{2,6},{6,2},{3,7},{7,3},{8,12},{12,8},{9,1... | collective-permute-start | bytes 1572872 | tf_op jit(solution)/shard_map/ppermute | solution.py:292
  1.2 10.2 %copy-start = (bf16[1024,256]{1,0:T(8,128)(2,1)S(1)}, bf16[1024,256]{1,0:T(8,128)(2,1)}, u32[]{:S(2)}) copy-start(bf16[1024,256]{1,0:T(8,128)(2,1)} %refs_3_.5) | copy-start | bytes 1572868
  1.2 10.2 %copy-start.1 = (bf16[256,1024]{1,0:T(8,128)(2,1)S(1)}, bf16[256,1024]{1,0:T(8,128)(2,1)}, u32[]{:S(2)}) copy-start(bf16[256,1024]{1,0:T(8,128)(2,1)} %refs_3_.4) | copy-start | bytes 1572868
  2.9 4.9 %collective-permute-start = (bf16[16,1152]{1,0:T(8,128)(2,1)S(1)}, bf16[16,1152]{1,0:T(8,128)(2,1)S(1)}, u32[]{:S(2)}, u32[]{:S(2)}) collective-permute-start(bf16[16,1152]{1,0:T(8,128)(2,1)S(1)} %get-tuple-element.21.refs_0_), channel_id=1, source_target_pairs={{0,8},{8,0},{16,24},{24,16},{1,9},{9,1},{17,25},{25,17},{2,10},{10... | collective-permute-start | bytes 110600 | tf_op jit(solution)/shard_map/ppermute | solution.py:292
  5.9 4.9 %collective-permute-start.2 = (bf16[16,1152]{1,0:T(8,128)(2,1)S(1)}, bf16[16,1152]{1,0:T(8,128)(2,1)S(1)}, u32[]{:S(2)}, u32[]{:S(2)}) collective-permute-start(bf16[16,1152]{1,0:T(8,128)(2,1)S(1)} %get-tuple-element.22), channel_id=1, source_target_pairs={{0,24},{8,16},{16,8},{24,0},{1,25},{9,17},{17,9},{25,1},{2,26},{10... | collective-permute-start | bytes 110600 | tf_op jit(solution)/shard_map/ppermute | solution.py:292
  7.4 4.0 %collective-permute-start.1 = (bf16[16,1152]{1,0:T(8,128)(2,1)S(1)}, bf16[16,1152]{1,0:T(8,128)(2,1)S(1)}, u32[]{:S(2)}, u32[]{:S(2)}) collective-permute-start(bf16[16,1152]{1,0:T(8,128)(2,1)S(1)} %get-tuple-element.22), channel_id=1, source_target_pairs={{0,16},{8,24},{16,0},{24,8},{1,17},{9,25},{17,1},{25,9},{2,18},{10... | collective-permute-start | bytes 110600 | tf_op jit(solution)/shard_map/ppermute | solution.py:292
  12.2 4.4 %collective-permute-start.6 = (s16[32,1152]{1,0:T(8,128)(2,1)S(1)}, s16[32,1152]{1,0:T(8,128)(2,1)S(1)}, u32[]{:S(2)}, u32[]{:S(2)}) collective-permute-start(s16[32,1152]{1,0:T(8,128)(2,1)S(1)} %get-tuple-element.23.refs_0_), channel_id=1, source_target_pairs={{0,1},{1,0},{2,3},{3,2},{4,5},{5,4},{6,7},{7,6},{8,9},{9,8},{10,11... | collective-permute-start | bytes 221192 | tf_op jit(solution)/shard_map/ppermute | solution.py:292
  13.8 12.4 %collective-permute-start.3 = (bf16[64,1152]{1,0:T(8,128)(2,1)S(1)}, bf16[64,1152]{1,0:T(8,128)(2,1)S(1)}, u32[]{:S(2)}, u32[]{:S(2)}) collective-permute-start(bf16[64,1152]{1,0:T(8,128)(2,1)S(1)} %shard_map.94.refs_0_), channel_id=1, source_target_pairs={{0,4},{4,0},{1,5},{5,1},{2,6},{6,2},{3,7},{7,3},{8,12},{12,8},{9,1... | collective-permute-start | bytes 442376 | tf_op jit(solution)/shard_map/ppermute | solution.py:292
  16.8 5.3 %collective-permute-start.7 = (s16[32,1152]{1,0:T(8,128)(2,1)S(1)}, s16[32,1152]{1,0:T(8,128)(2,1)S(1)}, u32[]{:S(2)}, u32[]{:S(2)}) collective-permute-start(s16[32,1152]{1,0:T(8,128)(2,1)S(1)} %shard_map.96.refs_0_), channel_id=1, source_target_pairs={{0,2},{1,3},{2,0},{3,1},{4,6},{5,7},{6,4},{7,5},{8,10},{9,11},{10,... | collective-permute-start | bytes 221192 | tf_op jit(solution)/shard_map/ppermute | solution.py:292
  22.5 3.6 %collective-permute-start.8 = (bf16[64,256]{1,0:T(8,128)(2,1)S(1)}, bf16[64,256]{1,0:T(8,128)(2,1)S(1)}, u32[]{:S(2)}, u32[]{:S(2)}) collective-permute-start(bf16[64,256]{1,0:T(8,128)(2,1)S(1)} %get-tuple-element.26), channel_id=1, source_target_pairs={{0,4},{4,0},{1,5},{5,1},{2,6},{6,2},{3,7},{7,3},{8,12},{12,8},{9,1... | collective-permute-start | bytes 98312 | tf_op jit(solution)/shard_map/ppermute | solution.py:292
  22.6 5.2 %collective-permute-start.9 = (bf16[8,1152]{1,0:T(8,128)(2,1)S(1)}, bf16[8,1152]{1,0:T(8,128)(2,1)S(1)}, u32[]{:S(2)}, u32[]{:S(2)}) collective-permute-start(bf16[8,1152]{1,0:T(8,128)(2,1)S(1)} %get-tuple-element.29), channel_id=1, source_target_pairs={{0,8},{8,0},{16,24},{24,16},{1,9},{9,1},{17,25},{25,17},{2,10},{10... | collective-permute-start | bytes 55304 | tf_op jit(solution)/shard_map/ppermute | solution.py:292
  24.2 3.8 %collective-permute-start.10 = (bf16[8,1152]{1,0:T(8,128)(2,1)S(1)}, bf16[8,1152]{1,0:T(8,128)(2,1)S(1)}, u32[]{:S(2)}, u32[]{:S(2)}) collective-permute-start(bf16[8,1152]{1,0:T(8,128)(2,1)S(1)} %get-tuple-element.30), channel_id=1, source_target_pairs={{0,16},{8,24},{16,0},{24,8},{1,17},{9,25},{17,1},{25,9},{2,18},{10... | collective-permute-start | bytes 55304 | tf_op jit(solution)/shard_map/ppermute | solution.py:292
  24.7 4.7 %collective-permute-start.11 = (bf16[8,1152]{1,0:T(8,128)(2,1)S(1)}, bf16[8,1152]{1,0:T(8,128)(2,1)S(1)}, u32[]{:S(2)}, u32[]{:S(2)}) collective-permute-start(bf16[8,1152]{1,0:T(8,128)(2,1)S(1)} %get-tuple-element.31), channel_id=1, source_target_pairs={{0,24},{8,16},{16,8},{24,0},{1,25},{9,17},{17,9},{25,1},{2,26},{10... | collective-permute-start | bytes 55304 | tf_op jit(solution)/shard_map/ppermute | solution.py:292
